TPU v7x, 128 devices: a whole 4x4x4 slice. The times are simulated.
128 devices in a mesh: ctx: 128 (over x, z, y, core).
Axes of the slice: x: 4, y: 4, z: 4, core: 2. Of those that a mesh axis runs over, the one named last changes fastest.
Arguments:
- inputs: bfloat16 [16384, 4096], P('ctx'), may hold values from -24 to 24
- streams: bfloat16 [3, 4096, 16384], P(None, None, 'ctx'), may hold values from -6 to 6
- short_filter: float32 [3, 3, 4096], replicated, may hold values from -3.5 to 3.5
- long_filter: float32 [4096, 16384], P('ctx'), may hold values from -0.046875 to 0.046875
- skip_gain: float32 [4096], P('ctx'), may hold values from -4 to 4
Outputs:
- gated: bfloat16 [4096, 16384], P(None, 'ctx')
- input_gram: float32 [512, 8, 512], P('ctx')
- output_gram: float32 [512, 8, 512], P('ctx')
All inputs are finite; a program needn't handle non-finite values.
Results may differ from a plain program's by a relative error of at most 0.0076.
Values may be sent and summed in bfloat16 or wider, within the bound.
A program may use at most 128 MiB of HBM per device.

v0:
```python
import math

import jax
import jax.numpy as jnp
from jax import lax
from jax.sharding import PartitionSpec as P

D = 4096
BLOCK = 512
SHORT = 3


HIGHEST_MODE = lax.Precision.HIGHEST


def shifted(block, axis, distance):
    devices = range(lax.axis_size(axis))
    route = [(i - distance, i) for i in devices if i - distance in devices]
    return lax.ppermute(block, axis, route)


def spectral_tables(seq_length):
    total = 2 * seq_length
    width_two = 256
    rows_one = total // width_two
    half_one = rows_one // 2
    index_one = jnp.arange(rows_one, dtype=jnp.int32)
    index_half = jnp.arange(half_one, dtype=jnp.int32)
    index_two = jnp.arange(width_two, dtype=jnp.int32)
    angle_one = (index_one[:, None] * index_half[None, :] % rows_one).astype(jnp.float32) * (
        2.0 * math.pi / rows_one
    )
    angle_two = (index_two[:, None] * index_two[None, :] % width_two).astype(jnp.float32) * (
        2.0 * math.pi / width_two
    )
    angle_turn = (index_one[:, None] * index_two[None, :] % total).astype(jnp.float32) * (
        2.0 * math.pi / total
    )
    return (
        jnp.cos(angle_one),
        -jnp.sin(angle_one),
        jnp.cos(angle_two),
        -jnp.sin(angle_two),
        jnp.cos(angle_turn),
        -jnp.sin(angle_turn),
    )


def forward_transform(signal, tables):
    cos_one, sin_one, cos_two, sin_two, turn_cos, turn_sin = tables
    first_re = jnp.einsum("scmn,km->sckn", signal, cos_one, precision=HIGHEST_MODE)
    first_im = jnp.einsum("scmn,km->sckn", signal, sin_one, precision=HIGHEST_MODE)
    turned_re = first_re * turn_cos - first_im * turn_sin
    turned_im = first_re * turn_sin + first_im * turn_cos
    spec_re = jnp.einsum("sckn,jn->sckj", turned_re, cos_two, precision=HIGHEST_MODE) - jnp.einsum(
        "sckn,jn->sckj", turned_im, sin_two, precision=HIGHEST_MODE
    )
    spec_im = jnp.einsum("sckn,jn->sckj", turned_re, sin_two, precision=HIGHEST_MODE) + jnp.einsum(
        "sckn,jn->sckj", turned_im, cos_two, precision=HIGHEST_MODE
    )
    return (spec_re, spec_im)


def inverse_transform(prod_re, prod_im, tables):
    cos_one, sin_one, cos_two, sin_two, turn_cos, turn_sin = tables
    back_re = jnp.einsum("ckj,jn->ckn", prod_re, cos_two, precision=HIGHEST_MODE) + jnp.einsum(
        "ckj,jn->ckn", prod_im, sin_two, precision=HIGHEST_MODE
    )
    back_im = jnp.einsum("ckj,jn->ckn", prod_im, cos_two, precision=HIGHEST_MODE) - jnp.einsum(
        "ckj,jn->ckn", prod_re, sin_two, precision=HIGHEST_MODE
    )
    untwist_re = back_re * turn_cos + back_im * turn_sin
    untwist_im = back_im * turn_cos - back_re * turn_sin
    return jnp.einsum("ckn,km->cmn", untwist_re, cos_one, precision=HIGHEST_MODE) + jnp.einsum(
        "ckn,km->cmn", untwist_im, sin_one, precision=HIGHEST_MODE
    )


def long_conv(product, long_filter, skip_gain):
    channels, seq_length = product.shape
    tables = spectral_tables(seq_length)
    half_one = tables[0].shape[1]
    values = product.astype(jnp.float32)
    stacked = jnp.stack([values, long_filter]).reshape(2, channels, half_one, 256)
    spec_re, spec_im = forward_transform(stacked, tables)
    prod_re = spec_re[0] * spec_re[1] - spec_im[0] * spec_im[1]
    prod_im = spec_re[0] * spec_im[1] + spec_im[0] * spec_re[1]
    signal = inverse_transform(prod_re, prod_im, tables).reshape(channels, seq_length)
    return (signal / (2 * seq_length) + skip_gain[:, None] * values).astype(jnp.bfloat16)


def body(inputs, streams, short_filter, long_filter, skip_gain):
    tok_count = streams.shape[2]
    shards = lax.axis_size("ctx")
    seq_length = tok_count * shards
    input_cols = inputs.reshape(tok_count, D // BLOCK, BLOCK)
    picked = input_cols
    input_gram = lax.psum_scatter(
        jnp.einsum("tbp,tbq->pbq", picked, input_cols, preferred_element_type=jnp.float32)
        / seq_length,
        "ctx",
        scatter_dimension=0,
        tiled=True,
    )
    edge = shifted(streams[:, :, tok_count - (SHORT - 1) :], "ctx", 1)
    padded = jnp.concatenate([edge, streams], axis=2)
    total = jnp.zeros(streams.shape, jnp.float32)
    for offset in range(SHORT):
        begin = SHORT - 1 - offset
        total = total + short_filter[:, offset, :, None] * padded[
            :, :, begin : begin + tok_count
        ].astype(jnp.float32)
    mixed = lax.optimization_barrier(total.astype(jnp.bfloat16))
    moved = lax.all_to_all(mixed, "ctx", split_axis=1, concat_axis=2, tiled=True)
    product = (moved[1].astype(jnp.float32) * moved[2].astype(jnp.float32)).astype(jnp.bfloat16)
    product = lax.optimization_barrier(product)
    conv = lax.optimization_barrier(long_conv(product, long_filter, skip_gain))
    gated_channels = (moved[0].astype(jnp.float32) * conv.astype(jnp.float32)).astype(jnp.bfloat16)
    gated = lax.all_to_all(gated_channels, "ctx", split_axis=1, concat_axis=0, tiled=True)
    gated_rows = gated.reshape(D // BLOCK, BLOCK, tok_count)
    picked = gated_rows
    output_gram = lax.psum_scatter(
        jnp.einsum("bpt,bqt->pbq", picked, gated_rows, preferred_element_type=jnp.float32)
        / seq_length,
        "ctx",
        scatter_dimension=0,
        tiled=True,
    )
    return (gated, input_gram, output_gram)


def solution(mesh):
    in_specs = (P("ctx", None), P(None, None, "ctx"), P(), P("ctx", None), P("ctx"))
    out_specs = (P(None, "ctx"), P("ctx", None, None), P("ctx", None, None))
    return jax.shard_map(body, mesh=mesh, in_specs=in_specs, out_specs=out_specs, check_vma=False)
```

profile of v0, /device:TPU:1, one launch (start us, length us, event | category | flops | bytes accessed | tf_op | source)
XLA Modules:
  0.0 1409.6 jit_solution(2606619993136974994)
XLA Ops:
  7.2 0.0 copy-start
  7.2 0.0 copy-start.5
  7.2 4.6 slice.48
  11.8 4.0 copy.101
  15.8 4.6 collective-permute-start
  20.4 0.0 copy-done.5
  20.4 0.1 fusion.142
  20.5 0.0 copy-done
  20.5 20.5 %copy.79 = bf16[3,4096,128]{2,0,1:T(4,128)(2,1)} copy(bf16[3,4096,128]{2,1,0:T(8,128)(2,1)S(1)} %copy-done) | data formatting | bytes 6291456 | tf_op args[1]
  41.0 0.6 copy.96
  41.7 2.0 copy.98
  43.7 2.0 copy.97
  45.6 0.0 collective-permute-done
  45.7 4.7 copy.82
  50.3 25.2 %add_convert_fusion = bf16[3,4096,128]{2,0,1:T(4,128)(2,1)} fusion(bf16[3,4096,128]{2,0,1:T(4,128)(2,1)} %copy.79, bf16[3,4096,2]{2,0,1:T(4,128)(2,1)} %copy.82, f32[3,4096]{0,1:T(8,128)} %bitcast.132, f32[3,4096]{0,1:T(8,128)} %bitcast.133, f32[3,4096]{0,1:T(8,128)S(1)} %bitcast.131), kind=kLoop, calls=%fused_computation.14 | loop fusion | flops 23592960 | bytes 6488064 | tf_op jit(solution)/shard_map/convert_element_type | solution.py:113
  75.5 0.0 copy-start.4
  75.5 10.3 all-to-all-start
  85.8 0.0 reduce-scatter.3.cloned.1.call-start
  85.9 0.0 copy-done.4
  85.9 4.5 multiply_bitcast_fusion.1
  90.4 10.5 copy.90
  100.9 0.0 reduce-scatter.3.cloned.1.call-update
  100.9 0.5 reduce-scatter.5.cloned.1.call-start
  101.4 2.2 copy.107
  103.6 0.5 sine_negate_fusion.5
  104.2 34.6 %all-to-all-done = bf16[3,4096,128]{2,0,1:T(4,128)(2,1)} async-done(((bf16[3,4096,128]{2,0,1:T(4,128)(2,1)}), bf16[3,4096,128]{2,0,1:T(4,128)(2,1)}, u32[]{:S(2)}, u32[]{:S(2)}) %all-to-all-start) | async-done | bytes 3145760 | tf_op jit(solution)/shard_map/all_to_all | solution.py:114
  138.8 4.8 copy.120
  143.6 0.0 copy-start.1
  143.6 0.4 multiply_convert_fusion
  144.0 0.7 copy.121
  144.6 0.0 copy-start.2
  144.7 0.3 copy.106
  144.9 0.3 copy-done.1
  145.3 0.3 copy-done.2
  145.6 0.2 bitcast_dynamic-update-slice_fusion.1
  145.8 0.1 bitcast_dynamic-update-slice_fusion
  146.0 7.4 fusion.80
  153.3 7.2 fusion.82
  160.5 11.3 fusion
  171.9 13.3 fusion.28
  185.2 11.5 fusion.2
  196.7 13.4 fusion.25
  210.1 6.7 multiply_subtract_fusion.1
  216.8 4.6 fusion.9
  221.4 4.6 fusion.11
  226.0 5.0 fusion.34
  231.0 4.6 fusion.31
  235.6 3.1 fusion.17
  238.8 3.5 add_multiply_fusion
  242.2 0.0 copy-start.3
  242.2 0.0 copy-start.6
  242.3 1.2 copy.108
  243.5 0.0 copy-done.3
  243.5 0.0 copy-done.6
  243.5 0.3 add_convert_fusion.1
  243.8 1.5 slice_convert_fusion
  245.3 1.2 copy_bitcast_fusion.2
  246.5 25.5 %all_to_all.34 = bf16[32,128,128]{2,0,1:T(8,128)(2,1)S(1)} all-to-all(bf16[32,128,128]{2,0,1:T(8,128)(2,1)S(1)} %copy_bitcast_fusion.2), channel_id=1, replica_groups=mesh['ctx'=128] {'ctx'}, dimensions={1} | all-to-all | bytes 2097152 | tf_op jit(solution)/shard_map/all_to_all | solution.py:119
  272.0 4.5 multiply_bitcast_fusion
  276.5 10.4 copy.91
  286.9 0.0 reduce-scatter.5.cloned.1.call-update
  287.0 467.4 %reduce-scatter.3.cloned.1.call-done = f32[4,8,512]{2,1,0:T(8,128)} async-done(((f32[512,8,512]{2,1,0:T(8,128)}), f32[4,8,512]{2,1,0:T(8,128)}) %reduce-scatter.3.cloned.1.call-update) | async-done | bytes 65552 | tf_op jit(solution)/shard_map/reduce_scatter | solution.py:98
  754.4 647.0 %reduce-scatter.5.cloned.1.call-done = f32[4,8,512]{2,1,0:T(8,128)} async-done(((f32[512,8,512]{2,1,0:T(8,128)}), f32[4,8,512]{2,1,0:T(8,128)}) %reduce-scatter.5.cloned.1.call-update) | async-done | bytes 65552 | tf_op jit(solution)/shard_map/reduce_scatter | solution.py:122
  1401.3 1.0 copy.124
Async XLA Ops:
  7.2 13.4 copy-start
  7.2 13.2 copy-start.5
  15.8 29.8 %collective-permute-start = (bf16[3,4096,2]{1,0,2:T(4,128)(2,1)}, bf16[3,4096,2]{1,0,2:T(4,128)(2,1)S(1)}, u32[]{:S(2)}, u32[]{:S(2)}) collective-permute-start(bf16[3,4096,2]{1,0,2:T(4,128)(2,1)} %copy.101), channel_id=1, source_target_pairs={{0,1},{1,2},{2,3},{3,4},{4,5},{5,6},{6,7},{7,8},{8,9},{9,10},{10,1... | collective-permute-start | bytes 147464 | tf_op jit(solution)/shard_map/ppermute | solution.py:19
  75.5 10.3 copy-start.4
  75.5 63.3 %all-to-all-start = ((bf16[3,4096,128]{2,0,1:T(4,128)(2,1)}), bf16[3,4096,128]{2,0,1:T(4,128)(2,1)}, u32[]{:S(2)}, u32[]{:S(2)}) async-start(bf16[3,4096,128]{2,0,1:T(4,128)(2,1)} %add_convert_fusion), calls=%async_computation | async-start | bytes 8388608 | tf_op jit(solution)/shard_map/all_to_all | solution.py:114
  85.8 668.6 %reduce-scatter.3.cloned.1.call-start = ((), (), s32[]{:S(2)}) async-start(), calls=%async_computation.4 | async-start | bytes 8454144 | tf_op jit(solution)/shard_map/reduce_scatter | solution.py:98
  100.9 1300.5 %reduce-scatter.5.cloned.1.call-start = ((), (), s32[]{:S(2)}) async-start(), calls=%async_computation.5 | async-start | bytes 8454144 | tf_op jit(solution)/shard_map/reduce_scatter | solution.py:122
  143.6 1.7 copy-start.1
  144.6 1.0 copy-start.2
  242.2 1.3 copy-start.3
  242.2 1.2 copy-start.6
Sparse Core Ops, SparseCore 0:
  101.0 653.3 reduce-scatter.2
  757.4 643.8 reduce-scatter.4
where the time goes:
time: 1420 us; the launch traced here: 1410 us
  waiting for transfers between devices  1150 us (81%)
  matrix products  98.5 us (7%)
  local copies, waits for them, and re-layouts  70.6 us (5%)
  other arithmetic  35.8 us (3%)
  blocking collectives  25.5 us (2%)
  starting transfers between devices  15.4 us (1%)
  between operations  14.8 us (1%)
    reduce_scatter x1, waiting for transfers between devices, body(): lax.psum_scatter(jnp.einsum('bpt,bqt->pbq', picked, gated_rows, preferred...  647 us
    reduce_scatter x1, waiting for transfers between devices, body(): lax.psum_scatter(jnp.einsum('tbp,tbq->pbq', picked, input_cols, preferred...  467 us
    all_to_all x1, waiting for transfers between devices, body(): lax.all_to_all(mixed, 'ctx', split_axis=1, concat_axis=2, tiled=True)  34.6 us
    unnamed x22, local copies, waits for them, and re-layouts  30.8 us
  transfers between devices with their start and end apart: 4, of which 3 were waited for; matrix products, arithmetic and copies ran while one was open for 12% of the time, Pallas kernels for 0%

commit v1 on v0

v1 whole, which is shorter than its diff:
```python
import math

import jax
import jax.numpy as jnp
import numpy as np
from jax import lax
from jax.experimental import pallas as pl
from jax.experimental.pallas import tpu as pltpu
from jax.sharding import PartitionSpec as P

D = 4096
BLOCK = 512
SHORT = 3
DEVICES = 128
BLOCKS = D // BLOCK
PLACES = DEVICES // BLOCKS
OWN = D // DEVICES
SIDE = 128
F32 = jnp.float32
BF16 = jnp.bfloat16
MESH = pl.DeviceIdType.MESH


def member_of(block, group):
    return 16 * block + 8 * ((group // 8 + block) % 2) + group % 8


def split(values):
    high = np.asarray(values, np.float32).astype(BF16)
    low = (values - high.astype(np.float64)).astype(np.float32).astype(BF16)
    return high, low


def tables():
    index = np.arange(SIDE)
    one = np.exp(2j * math.pi * np.outer(index + 0.25, index) / SIDE)
    turn = np.exp(2j * math.pi * np.outer(index + 0.25, index) / (SIDE * SIDE))
    two = np.exp(2j * math.pi * np.outer(index, index) / SIDE)
    order = np.array([member_of(u, j) for j in range(PLACES) for u in range(BLOCKS)])
    stacked = np.concatenate([one.real, one.imag], 0)
    high, low = split(stacked)
    one_x = np.concatenate([high[:, order], low[:, order]], 1)
    one_h = np.concatenate([high, low, high], 1)
    ahead = np.block([[two.real, two.imag], [-two.imag, two.real]])
    back = np.block([[two.real, -two.imag], [two.imag, two.real]])
    high, low = split(ahead)
    two_x = np.concatenate([high, high, low], 0)
    high, low = split(back)
    two_y = np.concatenate([high, high, low], 0)
    last = stacked.T[order] / (SIDE * SIDE)
    high, low = split(last)
    one_y = np.concatenate([high, low, high], 1)
    turn_re = np.tile(turn.real, (1, 2)).astype(np.float32)
    turn_im = np.tile(turn.imag, (1, 2)).astype(np.float32)
    edge = np.zeros((SHORT, 16, SIDE), np.float32)
    for s in range(SHORT):
        edge[s, 2 * s, SIDE - 2] = 1
        edge[s, 2 * s + 1, SIDE - 1] = 1
    return one_x, one_h, two_x, two_y, one_y, turn_re, turn_im, edge.astype(BF16)


def halves(values):
    high = values.astype(BF16)
    low = (values - high.astype(F32)).astype(BF16)
    return high, low


def dot(left, right, dims=((1,), (0,))):
    return lax.dot_general(left, right, (dims, ((), ())), preferred_element_type=F32)


def kernel(
    inputs, streams, taps, filters, gain, one_x, one_h, two_x, two_y, one_y, turn_re, turn_im, edge_at,
    gated, input_gram, output_gram,
    x_own, h_own, taps_rows, taps_cols, edge_out, edge_in,
    p_out, p_in, q_out, q_in, i_in,
    r_in, r_rows, h_rows, h_spec, y_rows, y_out, c_in,
    g_out, g_cols, part_out, part_in, fin_out, fin_in,
    local_sem, edge_sem, group_send, group_recv, block_send, block_recv, fin_send, fin_recv,
):
    me = lax.axis_index("ctx")
    block = lax.div(me, 16)
    place = lax.rem(me, 16)
    group = 8 * lax.rem(lax.div(place, 8) + block, 2) + lax.rem(place, 8)

    def member(b, j):
        return 16 * b + 8 * lax.rem(lax.div(j, 8) + b, 2) + lax.rem(j, 8)

    def remote(src, dst, send, recv, device):
        return pltpu.make_async_remote_copy(
            src_ref=src, dst_ref=dst, send_sem=send, recv_sem=recv, device_id=(device,), device_id_type=MESH
        )

    stream_copies = [
        pltpu.make_async_copy(streams.at[s], x_own.at[s], local_sem.at[s]) for s in range(SHORT)
    ]
    for copy in stream_copies:
        copy.start()
    filter_copy = pltpu.make_async_copy(filters, h_own, local_sem.at[3])
    filter_copy.start()

    def columns(u):
        return pl.ds(pl.multiple_of(u * BLOCK, BLOCK), BLOCK)

    def input_copy(u, slot):
        return remote(inputs.at[:, columns(u)], i_in.at[slot], group_send.at[2, u], group_recv.at[2, slot], member(u, group))

    own_input = pltpu.make_async_copy(inputs.at[:, columns(block)], i_in.at[block], local_sem.at[4])
    own_input.start()

    @pl.loop(1, BLOCKS)
    def _(r):
        input_copy(lax.rem(block + r, BLOCKS), block).start()

    for copy in stream_copies:
        copy.wait()
    edge = dot(edge_at[0], x_own[0], ((1,), (1,)))
    edge += dot(edge_at[1], x_own[1], ((1,), (1,)))
    edge += dot(edge_at[2], x_own[2], ((1,), (1,)))
    edge_out[...] = edge.astype(BF16)

    edge_copy = remote(edge_out, edge_in, edge_sem.at[0], edge_sem.at[1], lax.rem(me + 1, DEVICES))

    @pl.when(me < DEVICES - 1)
    def _():
        edge_copy.start()

    taps_rows[...] = jnp.zeros_like(taps_rows)
    for s in range(SHORT):
        taps_rows[SHORT * s : SHORT * s + SHORT, :] = taps[s]
    for k in range(D // SIDE):
        taps_cols[k * SIDE : (k + 1) * SIDE, :] = taps_rows[:, k * SIDE : (k + 1) * SIDE].T

    filter_copy.wait()
    for m in range(SIDE):
        h_rows[m * OWN : (m + 1) * OWN, :] = h_own[:, m * SIDE : (m + 1) * SIDE]

    @pl.when(me == 0)
    def _():
        edge_in[...] = jnp.zeros_like(edge_in)

    @pl.when(me > 0)
    def _():
        edge_copy.wait_recv()

    lane = lax.broadcasted_iota(jnp.int32, (SIDE, SIDE), 1)

    def mixed(s, row):
        row = pl.multiple_of(row, SIDE)
        here = x_own[s, pl.ds(row, SIDE), :].astype(F32)
        before = dot(edge_in[:, pl.ds(row, SIDE)], edge_at[s], ((0,), (0,)))
        one = pltpu.roll(jnp.where(lane >= SIDE - 1, before, here), 1, 1)
        two = pltpu.roll(jnp.where(lane >= SIDE - 2, before, here), 2, 1)
        col = taps_cols[pl.ds(row, SIDE), :]
        total = col[:, 3 * s : 3 * s + 1] * here
        total = total + col[:, 3 * s + 1 : 3 * s + 2] * one
        total = total + col[:, 3 * s + 2 : 3 * s + 3] * two
        return total.astype(BF16)

    def product_copy(u, slot):
        return remote(p_out.at[u], p_in.at[slot], group_send.at[0, u], group_recv.at[0, slot], member(u, group))

    def query_copy(u, slot):
        return remote(q_out.at[u], q_in.at[slot], group_send.at[1, u], group_recv.at[1, slot], member(u, group))

    def fill_product(ref, u):
        @pl.loop(0, BLOCK // SIDE)
        def _(k):
            row = u * BLOCK + k * SIDE
            value = mixed(1, row).astype(F32) * mixed(2, row).astype(F32)
            ref[pl.ds(pl.multiple_of(k * SIDE, SIDE), SIDE), :] = value.astype(BF16)

    def fill_query(ref, u):
        @pl.loop(0, BLOCK // SIDE)
        def _(k):
            ref[pl.ds(pl.multiple_of(k * SIDE, SIDE), SIDE), :] = mixed(0, u * BLOCK + k * SIDE)

    @pl.loop(1, BLOCKS)
    def _(r):
        u = lax.rem(block + r, BLOCKS)
        fill_product(p_out.at[u], u)
        product_copy(u, block).start()

    fill_product(p_in.at[block], block)

    @pl.loop(1, BLOCKS)
    def _(r):
        u = lax.rem(block + r, BLOCKS)
        fill_query(q_out.at[u], u)
        query_copy(u, block).start()

    fill_query(q_in.at[block], block)

    @pl.loop(1, BLOCKS)
    def _(r):
        u = lax.rem(block + r, BLOCKS)
        product_copy(u, u).wait_recv()

    def rows_of(o, size):
        return pl.ds(pl.multiple_of(o * size, size), size)

    def owner_copy(o, slot):
        return remote(
            p_in.at[:, rows_of(o, OWN), :], r_in.at[slot], block_send.at[0, o], block_recv.at[0, slot], 16 * block + o
        )

    @pl.loop(1, PLACES)
    def _(r):
        owner_copy(lax.rem(place + r, PLACES), group).start()

    own_product = pltpu.make_async_copy(p_in.at[:, rows_of(place, OWN), :], r_in.at[group], local_sem.at[5])
    own_product.start()

    def pair(ref, c):
        return [ref[pl.ds(c + k, SIDE, stride=OWN), :] for k in range(2)]

    def turned(values, sign):
        re, im = values[:SIDE], values[SIDE:]
        cos, sin = turn_re[...], sign * turn_im[...]
        return re * cos - im * sin, re * sin + im * cos

    def swapped(re, im):
        return jnp.concatenate(
            [jnp.concatenate([v[:, k * SIDE : (k + 1) * SIDE] for v in (re, im)], 1) for k in range(2)], 0
        )

    def three(values, axis):
        high, low = halves(values)
        return jnp.concatenate([high, low, high] if axis else [high, high, low], axis)

    @pl.loop(0, OWN // 2)
    def _(k):
        c = 2 * k
        values = jnp.concatenate(pair(h_rows, c), 1)
        first = dot(one_h[...], three(values, 0))
        spectrum = dot(three(swapped(*turned(first, 1.0)), 1), two_x[...])
        h_spec[pl.ds(pl.multiple_of(c * SIDE, 2 * SIDE), 2 * SIDE), :] = spectrum

    own_input.wait()

    @pl.loop(1, BLOCKS)
    def _(r):
        u = lax.rem(block + r, BLOCKS)
        input_copy(u, u).wait_recv()

    def part_copy(which, o, slot):
        return remote(
            part_out.at[which, rows_of(o, OWN), :],
            part_in.at[which, slot],
            block_send.at[2 + which, o],
            block_recv.at[2 + which, slot],
            16 * block + o,
        )

    def send_parts(which):
        @pl.loop(1, PLACES)
        def _(r):
            part_copy(which, lax.rem(place + r, PLACES), place).start()

        part_in[which, place] = part_out[which, rows_of(place, OWN), :]

    def sum_parts(which):
        @pl.loop(1, PLACES)
        def _(r):
            o = lax.rem(place + r, PLACES)
            part_copy(which, o, o).wait_recv()

        total = part_in[which, 0].astype(F32)
        for o in range(1, PLACES):
            total += part_in[which, o].astype(F32)
        total = total * (1.0 / (SIDE * SIDE))
        for i in range(BLOCKS):
            fin_out[which, i] = total[4 * i : 4 * i + 4]

    def fin_copy(which, i, slot, device):
        return remote(
            fin_out.at[which, i], fin_in.at[which, slot], fin_send.at[which, i], fin_recv.at[which, slot], device
        )

    def send_fin(which):
        @pl.loop(0, BLOCKS)
        def _(i):
            device = 8 * place + i

            @pl.when(device != me)
            def _():
                fin_copy(which, i, block, device).start()

            @pl.when(device == me)
            def _():
                fin_in[which, block] = fin_out[which, i]

    def wait_fin(which, out):
        @pl.loop(0, BLOCKS)
        def _(b):
            @pl.when(16 * b + lax.div(me, 8) != me)
            def _():
                fin_copy(which, 0, b, me).wait_recv()

        for r in range(4):
            out[r] = fin_in[which, :, r, :]

    rows = i_in[...].reshape(BLOCKS * SIDE, BLOCK)
    part_out[0] = dot(rows, rows, ((0,), (0,))).astype(BF16)
    send_parts(0)

    @pl.loop(1, PLACES)
    def _(r):
        j = lax.rem(group + r, PLACES)
        owner_copy(place, j).wait_recv()

    own_product.wait()

    @pl.loop(0, SIDE)
    def _(k):
        r_rows[rows_of(k, OWN), :] = r_in[lax.div(k, BLOCKS), lax.rem(k, BLOCKS)].astype(F32)

    @pl.loop(0, OWN // 2)
    def _(k):
        c = 2 * k
        values = pair(r_rows, c)
        exact = jnp.concatenate(values, 1).astype(BF16)
        first = dot(one_x[...], jnp.concatenate([exact, exact], 0))
        spectrum = dot(three(swapped(*turned(first, 1.0)), 1), two_x[...])
        other = h_spec[pl.ds(pl.multiple_of(c * SIDE, 2 * SIDE), 2 * SIDE), :]
        x_re, x_im, h_re, h_im = spectrum[:, :SIDE], spectrum[:, SIDE:], other[:, :SIDE], other[:, SIDE:]
        both = jnp.concatenate([x_re * h_re - x_im * h_im, x_re * h_im + x_im * h_re], 1)
        back = dot(three(both, 1), two_y[...])
        lanes = jnp.concatenate(
            [jnp.concatenate([back[q * SIDE : (q + 1) * SIDE, p * SIDE : (p + 1) * SIDE] for q in range(2)], 1) for p in range(2)],
            0,
        )
        signal = dot(one_y[...], three(jnp.concatenate(turned(lanes, -1.0), 0), 0))
        for q in range(2):
            y_rows[pl.ds(c + q, SIDE, stride=OWN), :] = signal[:, q * SIDE : (q + 1) * SIDE] + gain[c + q] * values[q]

    def conv_copy(j, slot):
        return remote(
            y_out.at[j], c_in.at[slot], block_send.at[1, j], block_recv.at[1, slot], member(block, j)
        )

    @pl.loop(0, PLACES)
    def _(r):
        j = lax.rem(group + 1 + r, PLACES)
        for u in range(BLOCKS):
            y_out[j, u] = y_rows[rows_of(j * BLOCKS + u, OWN), :].astype(BF16)

        @pl.when(r < PLACES - 1)
        def _():
            conv_copy(j, place).start()

    c_in[place] = y_out[group]
    sum_parts(0)
    send_fin(0)

    @pl.loop(1, BLOCKS)
    def _(r):
        u = lax.rem(block + r, BLOCKS)
        query_copy(u, u).wait_recv()

    @pl.loop(1, PLACES)
    def _(r):
        o = lax.rem(place + r, PLACES)
        conv_copy(group, o).wait_recv()

    def gated_copy(u, slot):
        return remote(
            g_out.at[u], gated.at[columns(slot), :], group_send.at[3, u], group_recv.at[3, slot], member(u, group)
        )

    def fill_gated(u):
        conv = c_in[:, u].reshape(BLOCK, SIDE).astype(F32)
        value = (q_in[u].astype(F32) * conv).astype(BF16)
        g_out[u] = value
        g_cols[:, pl.ds(pl.multiple_of(u * SIDE, SIDE), SIDE)] = value

    @pl.loop(1, BLOCKS)
    def _(r):
        u = lax.rem(block + r, BLOCKS)
        fill_gated(u)
        gated_copy(u, block).start()

    fill_gated(block)
    own_gated = pltpu.make_async_copy(g_out.at[block], gated.at[columns(block), :], local_sem.at[6])
    own_gated.start()

    part_out[1] = dot(g_cols[...], g_cols[...], ((1,), (1,))).astype(BF16)
    send_parts(1)
    wait_fin(0, input_gram)
    sum_parts(1)
    send_fin(1)
    wait_fin(1, output_gram)

    own_gated.wait()

    @pl.loop(1, BLOCKS)
    def _(r):
        u = lax.rem(block + r, BLOCKS)
        gated_copy(u, u).wait_recv()
        product_copy(u, u).wait_send()
        query_copy(u, u).wait_send()
        input_copy(u, u).wait_send()
        gated_copy(u, u).wait_send()

    @pl.loop(1, PLACES)
    def _(r):
        o = lax.rem(place + r, PLACES)
        owner_copy(o, o).wait_send()
        part_copy(0, o, o).wait_send()
        part_copy(1, o, o).wait_send()
        conv_copy(lax.rem(group + r, PLACES), o).wait_send()

    @pl.loop(0, BLOCKS)
    def _(i):
        @pl.when(8 * place + i != me)
        def _():
            fin_copy(0, i, i, me).wait_send()
            fin_copy(1, i, i, me).wait_send()

    @pl.when(me < DEVICES - 1)
    def _():
        edge_copy.wait_send()


def body(inputs, streams, short_filter, long_filter, skip_gain):
    anywhere = pl.BlockSpec(memory_space=pl.ANY)
    vmem = pl.BlockSpec(memory_space=pltpu.VMEM)
    smem = pl.BlockSpec(memory_space=pltpu.SMEM)
    constants = tables()
    dma = pltpu.SemaphoreType.DMA
    gram = jax.ShapeDtypeStruct((BLOCK // DEVICES, BLOCKS, BLOCK), F32)
    return pl.pallas_call(
        kernel,
        out_shape=(jax.ShapeDtypeStruct((D, SIDE), BF16), gram, gram),
        in_specs=[anywhere, anywhere, vmem, anywhere, smem] + [vmem] * len(constants),
        out_specs=(anywhere, vmem, vmem),
        scratch_shapes=[
            pltpu.VMEM((SHORT, D, SIDE), BF16),
            pltpu.VMEM((OWN, SIDE * SIDE), F32),
            pltpu.VMEM((16, D), F32),
            pltpu.VMEM((D, 16), F32),
            pltpu.VMEM((16, D), BF16),
            pltpu.VMEM((16, D), BF16),
            pltpu.VMEM((BLOCKS, BLOCK, SIDE), BF16),
            pltpu.VMEM((BLOCKS, BLOCK, SIDE), BF16),
            pltpu.VMEM((BLOCKS, BLOCK, SIDE), BF16),
            pltpu.VMEM((BLOCKS, BLOCK, SIDE), BF16),
            pltpu.VMEM((BLOCKS, SIDE, BLOCK), BF16),
            pltpu.VMEM((PLACES, BLOCKS, OWN, SIDE), BF16),
            pltpu.VMEM((SIDE * OWN, SIDE), F32),
            pltpu.VMEM((SIDE * OWN, SIDE), F32),
            pltpu.VMEM((OWN * SIDE, 2 * SIDE), F32),
            pltpu.VMEM((SIDE * OWN, SIDE), F32),
            pltpu.VMEM((PLACES, BLOCKS, OWN, SIDE), BF16),
            pltpu.VMEM((PLACES, BLOCKS, OWN, SIDE), BF16),
            pltpu.VMEM((BLOCKS, BLOCK, SIDE), BF16),
            pltpu.VMEM((BLOCK, BLOCKS * SIDE), BF16),
            pltpu.VMEM((2, BLOCK, BLOCK), BF16),
            pltpu.VMEM((2, PLACES, OWN, BLOCK), BF16),
            pltpu.VMEM((2, BLOCKS, 4, BLOCK), F32),
            pltpu.VMEM((2, BLOCKS, 4, BLOCK), F32),
            dma((8,)),
            dma((2,)),
            dma((4, BLOCKS)),
            dma((4, BLOCKS)),
            dma((4, PLACES)),
            dma((4, PLACES)),
            dma((2, BLOCKS)),
            dma((2, BLOCKS)),
        ],
        compiler_params=pltpu.CompilerParams(has_side_effects=True, vmem_limit_bytes=56 * 1024 * 1024),
    )(inputs, streams, short_filter, long_filter, skip_gain, *[jnp.asarray(c) for c in constants])


def solution(mesh):
    in_specs = (P("ctx", None), P(None, None, "ctx"), P(), P("ctx", None), P("ctx"))
    out_specs = (P(None, "ctx"), P("ctx", None, None), P("ctx", None, None))
    return jax.shard_map(body, mesh=mesh, in_specs=in_specs, out_specs=out_specs, check_vma=False)
```

time: 1420 us -> 129 us (0.09)
  waiting for transfers between devices: 1150 us -> 0 us
  Pallas kernels: 0 us -> 121 us
  matrix products: 98.5 us -> 0 us
  local copies, waits for them, and re-layouts: 70.6 us -> 5.21 us
  other arithmetic: 35.8 us -> 0 us
  blocking collectives: 25.5 us -> 0 us
  starting transfers between devices: 15.4 us -> 0 us
    reduce_scatter x2 -> x0, waiting for transfers between devices: 1110 us -> none  [the longest x1 647 us: body(): lax.psum_scatter(jnp.einsum('bpt,bqt->pbq', picked, gated_rows, preferred...]
    pallas_call x0 -> x1, Pallas kernels: none -> 121 us  [body(): pl.pallas_call(kernel, out_shape=(jax.ShapeDtypeStruct((D, SIDE), BF16),...]
    dot_general x14 -> x0, matrix products: 98.5 us -> none  [the longest x1 13.4 us: forward_transform(): jnp.einsum('sckn,jn->sckj', turned_re, cos_two, precision=HIGHEST_MODE)]
    all_to_all x1 -> x0, waiting for transfers between devices: 34.6 us -> none  [body(): lax.all_to_all(mixed, 'ctx', split_axis=1, concat_axis=2, tiled=True)]
    convert_element_type x4 -> x0, other arithmetic: 27.3 us -> none  [the longest x1 25.2 us: body(): mixed = lax.optimization_barrier(total.astype(jnp.bfloat16))]
    unnamed x22 -> x3, local copies, waits for them, and re-layouts: 30.8 us -> 5.21 us
    all_to_all x1 -> x0, blocking collectives: 25.5 us -> none  [body(): lax.all_to_all(gated_channels, 'ctx', split_axis=1, concat_axis=0, tiled=...]
    div x2 -> x0, local copies, waits for them, and re-layouts: 20.9 us -> none  [the longest x1 10.5 us: body(): jnp.einsum('tbp,tbq->pbq', picked, input_cols, preferred_element_type=jnp...]
  transfers between devices with their start and end apart: 4 -> 0, of which waited for: 3 -> 0; matrix products, arithmetic and copies ran while one was open for 12% -> 0% of each run, Pallas kernels for 0% -> 0%
where the time goes in v1:
time: 129 us; the launch traced here: 127 us
  Pallas kernels  121 us (94%)
  local copies, waits for them, and re-layouts  5.21 us (4%)
    pallas_call x1, Pallas kernels, body(): pl.pallas_call(kernel, out_shape=(jax.ShapeDtypeStruct((D, SIDE), BF16),...  121 us
    unnamed x3, local copies, waits for them, and re-layouts  5.21 us

profile of v1, /device:TPU:1, one launch (start us, length us, event | category | flops | bytes accessed | tf_op | source)
XLA Modules:
  0.0 126.8 jit_solution(13465393526581855356)
XLA Ops:
  0.6 121.0 %shard_map.148 = (bf16[4096,128]{1,0:T(8,128)(2,1)}, f32[4,8,512]{2,1,0:T(8,128)}, f32[4,8,512]{2,1,0:T(8,128)}) custom-call(bf16[128,4096]{1,0:T(8,128)(2,1)} %inputs.1, bf16[3,4096,128]{2,1,0:T(8,128)(2,1)} %streams.1, f32[3,3,4096]{2,1,0:T(4,128)} %taps.1, f32[32,16384]{1,0:T(8,128)} %filters.1, f32[32]{0:T(128)} %gain.1, ...), custom_call_target="tpu_custom_call" | custom-call | tf_op jit(solution)/shard_map/pallas_call | solution.py:432
  121.6 2.3 %copy.19 = bf16[4096,128]{1,0:T(8,128)(2,1)} copy(bf16[4096,128]{1,0:T(8,128)(2,1)} %get-tuple-element.6) | data formatting | bytes 2097152
  123.9 1.5 %copy.20 = f32[4,8,512]{2,1,0:T(8,128)} copy(f32[4,8,512]{2,1,0:T(8,128)} %get-tuple-element.7) | data formatting | bytes 131072
  125.4 1.5 %copy.21 = f32[4,8,512]{2,1,0:T(8,128)} copy(f32[4,8,512]{2,1,0:T(8,128)} %get-tuple-element.8) | data formatting | bytes 131072

commit v2 on v1

v2 whole, which is shorter than its diff:
```python
import math

import jax
import jax.numpy as jnp
import numpy as np
from jax import lax
from jax.experimental import pallas as pl
from jax.experimental.pallas import tpu as pltpu
from jax.sharding import PartitionSpec as P

D = 4096
BLOCK = 512
SHORT = 3
DEVICES = 128
BLOCKS = D // BLOCK
PLACES = DEVICES // BLOCKS
OWN = D // DEVICES
HALF = OWN // 2
SIDE = 128
PAIRS = 2
EARLY = 4
F32 = jnp.float32
BF16 = jnp.bfloat16
MESH = pl.DeviceIdType.MESH


def member_of(block, group):
    return 16 * block + 8 * ((group // 8 + block) % 2) + group % 8


def split(values):
    high = np.asarray(values, np.float32).astype(BF16)
    low = (values - high.astype(np.float64)).astype(np.float32).astype(BF16)
    return high, low


def tables():
    index = np.arange(SIDE)
    one = np.exp(2j * math.pi * np.outer(index + 0.25, index) / SIDE)
    turn = np.exp(2j * math.pi * np.outer(index + 0.25, index) / (SIDE * SIDE))
    two = np.exp(2j * math.pi * np.outer(index, index) / SIDE)
    order = np.array([member_of(u, j) for j in range(PLACES) for u in range(BLOCKS)])
    stacked = np.concatenate([one.real, one.imag], 0)
    high, low = split(stacked)
    one_x = np.concatenate([high[:, order], low[:, order]], 1)
    one_h = np.concatenate([high, low, high], 1)
    ahead = np.block([[two.real, two.imag], [-two.imag, two.real]])
    back = np.block([[two.real, -two.imag], [two.imag, two.real]])
    high, low = split(ahead)
    two_x = np.concatenate([high, high, low], 0)
    high, low = split(back)
    two_y = np.concatenate([high, high, low], 0)
    last = stacked.T[order] / (SIDE * SIDE)
    high, low = split(last)
    one_y = np.concatenate([high, low, high], 1)
    turn_re = np.tile(turn.real, (1, 2)).astype(np.float32)
    turn_im = np.tile(turn.imag, (1, 2)).astype(np.float32)
    pick = np.zeros((2, 2 * SIDE, SIDE), np.float32)
    pick[0, SIDE - 2, 0] = pick[0, SIDE - 1, 1] = pick[0, 2 * SIDE - 2, 2] = pick[0, 2 * SIDE - 1, 3] = 1
    pick[1, SIDE - 2, 0] = pick[1, SIDE - 1, 1] = 1
    shift = np.zeros((SHORT, 2 * SIDE, 2 * SIDE), np.float32)
    for s in range(SHORT):
        at = SIDE + (2 if s == 2 else 0)
        shift[s, index[:-1], index[1:]] = 1
        shift[s, index[:-2], SIDE + index[2:]] = 1
        shift[s, at + 1, 0] = shift[s, at, SIDE] = shift[s, at + 1, SIDE + 1] = 1
    return one_x, one_h, two_x, two_y, one_y, turn_re, turn_im, pick.astype(BF16), shift.astype(BF16)


def halves(values):
    high = values.astype(BF16)
    low = (values - high.astype(F32)).astype(BF16)
    return high, low


def three(values, axis):
    high, low = halves(values)
    return jnp.concatenate([high, low, high] if axis else [high, high, low], axis)


def dot(left, right, dims=((1,), (0,))):
    return lax.dot_general(left, right, (dims, ((), ())), preferred_element_type=F32)


def kernel(
    inputs, streams, taps, filters, gain, one_x, one_h, two_x, two_y, one_y, turn_re, turn_im, pick, shift,
    gated, sums,
    x_own, h_own, taps_rows, taps_cols, edge_out, edge_in, edge_wide,
    p_out, p_in, q_out, q_in, i_in,
    r_in, r_rows, h_rows, h_spec, y_rows, y_out, c_in,
    g_out, g_cols, part_out, part_in, fin_out,
    local_sem, edge_sem, group_send, group_recv, block_send, block_recv, fin_send, fin_recv,
):
    me = lax.axis_index("ctx")
    block = lax.div(me, 16)
    place = lax.rem(me, 16)
    group = 8 * lax.rem(lax.div(place, 8) + block, 2) + lax.rem(place, 8)

    def member(b, j):
        return 16 * b + 8 * lax.rem(lax.div(j, 8) + b, 2) + lax.rem(j, 8)

    def remote(src, dst, send, recv, device):
        return pltpu.make_async_remote_copy(
            src_ref=src, dst_ref=dst, send_sem=send, recv_sem=recv, device_id=(device,), device_id_type=MESH
        )

    def other_blocks(first=1, last=BLOCKS):
        def loop(step):
            pl.loop(first, last)(lambda r: step(lax.rem(block + r, BLOCKS)))

        return loop

    def other_places(step):
        pl.loop(1, PLACES)(lambda r: step(lax.rem(place + r, PLACES)))

    def other_groups(step):
        pl.loop(1, PLACES)(lambda r: step(lax.rem(group + r, PLACES)))

    barrier = pltpu.get_barrier_semaphore()

    def greet(device):
        pl.semaphore_signal(barrier, inc=1, device_id=(device,), device_id_type=MESH)

    other_blocks()(lambda u: greet(member(u, group)))
    other_places(lambda o: greet(16 * block + o))
    greet(lax.rem(me + 1, DEVICES))
    greet(lax.rem(me + DEVICES - 1, DEVICES))

    @pl.loop(0, BLOCKS)
    def _(i):
        @pl.when(8 * place + i != me)
        def _():
            greet(8 * place + i)

        @pl.when(16 * i + lax.div(me, 8) != me)
        def _():
            greet(16 * i + lax.div(me, 8))

    stream_copies = [
        pltpu.make_async_copy(streams.at[s], x_own.at[s], local_sem.at[s]) for s in range(SHORT)
    ]
    for s in (1, 2, 0):
        stream_copies[s].start()
    filter_copy = pltpu.make_async_copy(filters, h_own, local_sem.at[3])
    filter_copy.start()

    taps_rows[...] = jnp.zeros_like(taps_rows)
    for s in range(SHORT):
        taps_rows[SHORT * s : SHORT * s + SHORT, :] = taps[s]
    for k in range(D // SIDE):
        cols = taps_rows[:, k * SIDE : (k + 1) * SIDE].T
        taps_cols[k // 4, 4 * (k % 4) : 4 * (k % 4) + 4] = cols.reshape(4, 2, HALF, 16)

    def edge_copy(which):
        return remote(
            edge_out.at[which], edge_in.at[which], edge_sem.at[0, which], edge_sem.at[1, which], lax.rem(me + 1, DEVICES)
        )

    def eight(s, u, h, k):
        return x_own[s, u, 8 * k : 8 * k + 8, h].reshape(SIDE, SIDE)

    def fill_edge(which, width):
        edge = jnp.zeros((SIDE, SIDE), F32)
        for u in range(BLOCKS):
            for h in range(2):
                for k in range(2):
                    if which == 0:
                        got = dot(jnp.concatenate([eight(1, u, h, k), eight(2, u, h, k)], 1), pick[0])
                    else:
                        got = dot(eight(0, u, h, k), pick[1, :SIDE])
                    at = width * (4 * u + 2 * h + k)
                    edge += pltpu.roll(got, at, 1) if at else got
        edge_out[which] = edge.astype(BF16)

    stream_copies[1].wait()
    stream_copies[2].wait()
    fill_edge(0, 4)

    pl.semaphore_wait(barrier, 2 + BLOCKS - 1 + PLACES - 1 + 2 * BLOCKS - 2 * jnp.where(lax.div(me, 8) == place, 1, 0))

    @pl.when(me < DEVICES - 1)
    def _():
        edge_copy(0).start()

    def columns(u):
        return pl.ds(pl.multiple_of(u * BLOCK, BLOCK), BLOCK)

    def input_copy(u, slot):
        return remote(inputs.at[:, columns(u)], i_in.at[slot], group_send.at[2, u], group_recv.at[2, slot], member(u, group))

    own_input = pltpu.make_async_copy(inputs.at[:, columns(block)], i_in.at[block], local_sem.at[4])
    own_input.start()
    other_blocks(1, EARLY)(lambda u: input_copy(u, block).start())

    stream_copies[0].wait()
    fill_edge(1, 2)

    @pl.when(me < DEVICES - 1)
    def _():
        edge_copy(1).start()

    filter_copy.wait()
    for m in range(SIDE):
        h_rows[m * OWN : (m + 1) * OWN, :] = h_own[:, m * SIDE : (m + 1) * SIDE]

    def take_edge(which):
        @pl.when(me == 0)
        def _():
            edge_in[which] = jnp.zeros((SIDE, SIDE), BF16)

        @pl.when(me > 0)
        def _():
            edge_copy(which).wait_recv()

        edge_wide[which] = edge_in[which].astype(F32)

    def mixed(s, u, h, k, edge):
        here = eight(s, u, h, k)
        moved = dot(jnp.concatenate([here, edge], 1), shift[s])
        col = taps_cols[u, 8 * k : 8 * k + 8, h].reshape(SIDE, 16)
        total = col[:, 3 * s : 3 * s + 1] * here.astype(F32)
        total = total + col[:, 3 * s + 1 : 3 * s + 2] * moved[:, :SIDE]
        total = total + col[:, 3 * s + 2 : 3 * s + 3] * moved[:, SIDE:]
        return total.astype(BF16)

    def edge_of(which, width, u, h, k):
        at = lax.rem(SIDE - width * (4 * u + 2 * h + k), SIDE)
        return pltpu.roll(edge_wide[which], at, 1).astype(BF16)

    def product_copy(u, slot, h):
        return remote(p_out.at[u, h], p_in.at[slot, h], group_send.at[h, u], group_recv.at[h, slot], member(u, group))

    def query_copy(u, slot):
        return remote(q_out.at[u], q_in.at[slot], group_send.at[3, u], group_recv.at[3, slot], member(u, group))

    def fill_product(ref, u, h):
        for k in range(2):
            edge = edge_of(0, 4, u, h, k)
            value = mixed(1, u, h, k, edge).astype(F32) * mixed(2, u, h, k, edge).astype(F32)
            ref[8 * k : 8 * k + 8] = value.astype(BF16).reshape(8, HALF, SIDE)

    def fill_query(ref, u):
        for h in range(2):
            for k in range(2):
                value = mixed(0, u, h, k, edge_of(1, 2, u, h, k))
                ref[h, 8 * k : 8 * k + 8] = value.reshape(8, HALF, SIDE)

    take_edge(0)

    for h in range(2):
        @other_blocks()
        def _(u):
            fill_product(p_out.at[u, h], u, h)
            product_copy(u, block, h).start()

        fill_product(p_in.at[block, h], block, h)

    take_edge(1)

    @other_blocks()
    def _(u):
        fill_query(q_out.at[u], u)
        query_copy(u, block).start()

    fill_query(q_in.at[block], block)
    other_blocks(EARLY)(lambda u: input_copy(u, block).start())

    def pair(ref, c, stride):
        return [ref[pl.ds(c + k, SIDE, stride=stride), :] for k in range(2)]

    def turned(values, sign):
        re, im = values[:SIDE], values[SIDE:]
        cos, sin = turn_re[...], sign * turn_im[...]
        return re * cos - im * sin, re * sin + im * cos

    def swapped(re, im):
        return jnp.concatenate(
            [jnp.concatenate([v[:, k * SIDE : (k + 1) * SIDE] for v in (re, im)], 1) for k in range(2)], 0
        )

    def spectrum_rows(c):
        return pl.ds(pl.multiple_of(c * SIDE, 2 * SIDE), 2 * SIDE)

    def filter_half(h):
        @pl.loop(0, HALF // (2 * PAIRS))
        def _(step):
            starts = [h * HALF + 2 * (PAIRS * step + q) for q in range(PAIRS)]
            values = [jnp.concatenate(pair(h_rows, c, OWN), 1) for c in starts]
            first = [dot(one_h[...], three(v, 0)) for v in values]
            second = [dot(three(swapped(*turned(v, 1.0)), 1), two_x[...]) for v in first]
            for c, v in zip(starts, second):
                h_spec[spectrum_rows(c), :] = v

    def owner_copy(o, slot, h):
        return remote(
            p_in.at[:, h, o], r_in.at[h, slot], block_send.at[h, o], block_recv.at[h, slot], 16 * block + o
        )

    def own_product(h):
        return pltpu.make_async_copy(p_in.at[:, h, place], r_in.at[h, group], local_sem.at[5 + h])

    def forward(h):
        other_blocks()(lambda u: product_copy(u, u, h).wait_recv())
        other_places(lambda o: owner_copy(o, group, h).start())
        own_product(h).start()

    def conv_copy(j, slot, h):
        return remote(
            y_out.at[h, j], c_in.at[h, slot], block_send.at[2 + h, j], block_recv.at[2 + h, slot], member(block, j)
        )

    def convolve(h):
        other_groups(lambda j: owner_copy(place, j, h).wait_recv())
        own_product(h).wait()

        @pl.loop(0, PLACES)
        def _(j):
            for u in range(BLOCKS):
                at = pl.multiple_of((j * BLOCKS + u) * HALF, HALF)
                r_rows[pl.ds(at, HALF), :] = r_in[h, j, u].astype(F32)

        @pl.loop(0, HALF // (2 * PAIRS))
        def _(step):
            starts = [2 * (PAIRS * step + q) for q in range(PAIRS)]
            values = [pair(r_rows, c, HALF) for c in starts]
            exact = [jnp.concatenate(v, 1).astype(BF16) for v in values]
            first = [dot(one_x[...], jnp.concatenate([v, v], 0)) for v in exact]
            second = [dot(three(swapped(*turned(v, 1.0)), 1), two_x[...]) for v in first]
            third = []
            for c, v in zip(starts, second):
                other = h_spec[spectrum_rows(h * HALF + c), :]
                x_re, x_im, h_re, h_im = v[:, :SIDE], v[:, SIDE:], other[:, :SIDE], other[:, SIDE:]
                third.append(jnp.concatenate([x_re * h_re - x_im * h_im, x_re * h_im + x_im * h_re], 1))
            third = [dot(three(v, 1), two_y[...]) for v in third]
            third = [
                jnp.concatenate(
                    [
                        jnp.concatenate([v[q * SIDE : (q + 1) * SIDE, p * SIDE : (p + 1) * SIDE] for q in range(2)], 1)
                        for p in range(2)
                    ],
                    0,
                )
                for v in third
            ]
            signal = [dot(one_y[...], three(jnp.concatenate(turned(v, -1.0), 0), 0)) for v in third]
            for c, v, w in zip(starts, values, signal):
                for q in range(2):
                    y_rows[pl.ds(c + q, SIDE, stride=HALF), :] = (
                        w[:, q * SIDE : (q + 1) * SIDE] + gain[h * HALF + c + q] * v[q]
                    )

        def fill_conv(ref, j):
            for u in range(BLOCKS):
                at = pl.multiple_of((j * BLOCKS + u) * HALF, HALF)
                ref[u] = y_rows[pl.ds(at, HALF), :].astype(BF16)

        @other_groups
        def _(j):
            fill_conv(y_out.at[h, j], j)
            conv_copy(j, place, h).start()

        fill_conv(c_in.at[h, place], group)

    def part_rows(o):
        return pl.ds(pl.multiple_of(o * OWN, OWN), OWN)

    def part_copy(which, o, slot):
        return remote(
            part_out.at[which, part_rows(o), :],
            part_in.at[which, slot],
            block_send.at[4 + which, o],
            block_recv.at[4 + which, slot],
            16 * block + o,
        )

    def send_parts(which):
        other_places(lambda o: part_copy(which, o, place).start())
        part_in[which, place] = part_out[which, part_rows(place), :]

    def fin_copy(which, i, slot, device):
        return remote(
            fin_out.at[which, i], sums.at[which, slot], fin_send.at[which, i], fin_recv.at[which, slot], device
        )

    def sum_parts(which):
        other_places(lambda o: part_copy(which, o, o).wait_recv())
        total = part_in[which, 0].astype(F32)
        for o in range(1, PLACES):
            total += part_in[which, o].astype(F32)
        total = total * (1.0 / (SIDE * SIDE))
        for i in range(BLOCKS):
            fin_out[which, i] = total[4 * i : 4 * i + 4]

        @pl.loop(0, BLOCKS)
        def _(i):
            device = 8 * place + i

            @pl.when(device != me)
            def _():
                fin_copy(which, i, block, device).start()

            @pl.when(device == me)
            def _():
                sums[which, block] = fin_out[which, i]

    def wait_fin(which):
        @pl.loop(0, BLOCKS)
        def _(b):
            @pl.when(16 * b + lax.div(me, 8) != me)
            def _():
                fin_copy(which, 0, b, me).wait_recv()

    filter_half(0)
    forward(0)
    filter_half(1)
    forward(1)
    convolve(0)
    convolve(1)

    own_input.wait()
    other_blocks()(lambda u: input_copy(u, u).wait_recv())
    rows = i_in[...].reshape(BLOCKS * SIDE, BLOCK)
    part_out[0] = dot(rows, rows, ((0,), (0,))).astype(BF16)
    send_parts(0)

    def gated_copy(u, slot, h):
        return remote(
            g_out.at[u, h], gated.at[slot, :, h], group_send.at[4 + h, u], group_recv.at[4 + h, slot], member(u, group)
        )

    def own_gated(h):
        return pltpu.make_async_copy(g_out.at[block, h], gated.at[block, :, h], local_sem.at[7 + h])

    def fill_gated(u, h):
        value = (q_in[u, h].astype(F32) * c_in[h, :, u].astype(F32)).astype(BF16)
        g_out[u, h] = value
        g_cols[:, h, :, pl.ds(pl.multiple_of(u * SIDE, SIDE), SIDE)] = value

    other_blocks()(lambda u: query_copy(u, u).wait_recv())

    for h in range(2):
        other_places(lambda o: conv_copy(group, o, h).wait_recv())

        @other_blocks()
        def _(u):
            fill_gated(u, h)
            gated_copy(u, block, h).start()

        fill_gated(block, h)
        own_gated(h).start()

    columns_all = g_cols[...].reshape(BLOCK, BLOCKS * SIDE)
    part_out[1] = dot(columns_all, columns_all, ((1,), (1,))).astype(BF16)
    send_parts(1)
    sum_parts(0)
    sum_parts(1)
    wait_fin(0)
    wait_fin(1)

    for h in range(2):
        own_gated(h).wait()

    @other_blocks()
    def _(u):
        for h in range(2):
            gated_copy(u, u, h).wait_recv()
            gated_copy(u, u, h).wait_send()
            product_copy(u, u, h).wait_send()
        query_copy(u, u).wait_send()
        input_copy(u, u).wait_send()

    @other_places
    def _(o):
        for h in range(2):
            owner_copy(o, o, h).wait_send()
            part_copy(h, o, o).wait_send()

    @other_groups
    def _(j):
        for h in range(2):
            conv_copy(j, j, h).wait_send()

    @pl.loop(0, BLOCKS)
    def _(i):
        @pl.when(8 * place + i != me)
        def _():
            for which in range(2):
                fin_copy(which, i, i, me).wait_send()

    @pl.when(me < DEVICES - 1)
    def _():
        for which in range(2):
            edge_copy(which).wait_send()


def write_kernel(got, sums, gated, input_gram, output_gram, held, sems):
    def taken(b):
        return pltpu.make_async_copy(got.at[b], held.at[b], sems.at[0, b])

    def given(b):
        return pltpu.make_async_copy(held.at[b], gated.at[b], sems.at[1, b])

    for b in range(BLOCKS):
        taken(b).start()
    for r in range(BLOCK // DEVICES):
        input_gram[r] = sums[0, :, r, :]
        output_gram[r] = sums[1, :, r, :]
    for b in range(BLOCKS):
        taken(b).wait()
        given(b).start()
    for b in range(BLOCKS):
        given(b).wait()


def body(inputs, streams, short_filter, long_filter, skip_gain):
    anywhere = pl.BlockSpec(memory_space=pl.ANY)
    vmem = pl.BlockSpec(memory_space=pltpu.VMEM)
    smem = pl.BlockSpec(memory_space=pltpu.SMEM)
    constants = tables()
    dma = pltpu.SemaphoreType.DMA
    rows = BLOCK // DEVICES
    split_streams = streams.reshape(SHORT, BLOCKS, PLACES, 2, HALF, SIDE)
    got, sums = pl.pallas_call(
        kernel,
        out_shape=(
            jax.ShapeDtypeStruct((BLOCKS, PLACES, 2, HALF, SIDE), BF16),
            jax.ShapeDtypeStruct((2, BLOCKS, rows, BLOCK), F32),
        ),
        in_specs=[anywhere, anywhere, vmem, anywhere, smem] + [vmem] * len(constants),
        out_specs=(anywhere, vmem),
        scratch_shapes=[
            pltpu.VMEM((SHORT, BLOCKS, PLACES, 2, HALF, SIDE), BF16),
            pltpu.VMEM((OWN, SIDE * SIDE), F32),
            pltpu.VMEM((16, D), F32),
            pltpu.VMEM((BLOCKS, PLACES, 2, HALF, 16), F32),
            pltpu.VMEM((2, SIDE, SIDE), BF16),
            pltpu.VMEM((2, SIDE, SIDE), BF16),
            pltpu.VMEM((2, SIDE, SIDE), F32),
            pltpu.VMEM((BLOCKS, 2, PLACES, HALF, SIDE), BF16),
            pltpu.VMEM((BLOCKS, 2, PLACES, HALF, SIDE), BF16),
            pltpu.VMEM((BLOCKS, 2, PLACES, HALF, SIDE), BF16),
            pltpu.VMEM((BLOCKS, 2, PLACES, HALF, SIDE), BF16),
            pltpu.VMEM((BLOCKS, SIDE, BLOCK), BF16),
            pltpu.VMEM((2, PLACES, BLOCKS, HALF, SIDE), BF16),
            pltpu.VMEM((SIDE * HALF, SIDE), F32),
            pltpu.VMEM((SIDE * OWN, SIDE), F32),
            pltpu.VMEM((OWN * SIDE, 2 * SIDE), F32),
            pltpu.VMEM((SIDE * HALF, SIDE), F32),
            pltpu.VMEM((2, PLACES, BLOCKS, HALF, SIDE), BF16),
            pltpu.VMEM((2, PLACES, BLOCKS, HALF, SIDE), BF16),
            pltpu.VMEM((BLOCKS, 2, PLACES, HALF, SIDE), BF16),
            pltpu.VMEM((PLACES, 2, HALF, BLOCKS * SIDE), BF16),
            pltpu.VMEM((2, BLOCK, BLOCK), BF16),
            pltpu.VMEM((2, PLACES, OWN, BLOCK), BF16),
            pltpu.VMEM((2, BLOCKS, rows, BLOCK), F32),
            dma((9,)),
            dma((2, 2)),
            dma((6, BLOCKS)),
            dma((6, BLOCKS)),
            dma((6, PLACES)),
            dma((6, PLACES)),
            dma((2, BLOCKS)),
            dma((2, BLOCKS)),
        ],
        compiler_params=pltpu.CompilerParams(
            collective_id=0, has_side_effects=True, vmem_limit_bytes=56 * 1024 * 1024
        ),
    )(inputs, split_streams, short_filter, long_filter, skip_gain, *[jnp.asarray(c) for c in constants])
    gram = jax.ShapeDtypeStruct((rows, BLOCKS, BLOCK), F32)
    gated, input_gram, output_gram = pl.pallas_call(
        write_kernel,
        out_shape=(jax.ShapeDtypeStruct((BLOCKS, PLACES, 2, HALF, SIDE), BF16), gram, gram),
        in_specs=[anywhere, vmem],
        out_specs=(anywhere, vmem, vmem),
        scratch_shapes=[pltpu.VMEM((BLOCKS, PLACES, 2, HALF, SIDE), BF16), dma((2, BLOCKS))],
    )(got, sums)
    return gated.reshape(D, SIDE), input_gram, output_gram


def solution(mesh):
    in_specs = (P("ctx", None), P(None, None, "ctx"), P(), P("ctx", None), P("ctx"))
    out_specs = (P(None, "ctx"), P("ctx", None, None), P("ctx", None, None))
    return jax.shard_map(body, mesh=mesh, in_specs=in_specs, out_specs=out_specs, check_vma=False)
```

time: 129 us -> 88.7 us (0.69); the launches traced: 127 us -> 88.5 us
  Pallas kernels: 121 us -> 87.9 us
  local copies, waits for them, and re-layouts: 5.21 us -> 0 us
    pallas_call x1 -> x2, Pallas kernels: 121 us -> 87.9 us  [the longest x1 84.3 us: body(): pl.pallas_call(kernel, out_shape=(jax.ShapeDtypeStruct((BLOCKS, PLACES, 2...]
    unnamed x3 -> x0, local copies, waits for them, and re-layouts: 5.21 us -> none
where the time goes in v2:
time: 88.7 us; the launch traced here: 88.5 us
  Pallas kernels  87.9 us (99%)
    pallas_call x1, Pallas kernels, body(): pl.pallas_call(kernel, out_shape=(jax.ShapeDtypeStruct((BLOCKS, PLACES, 2...  84.3 us
    pallas_call x1, Pallas kernels, body(): pl.pallas_call(write_kernel, out_shape=(jax.ShapeDtypeStruct((BLOCKS, PLA...  3.64 us

profile of v2, /device:TPU:1, one launch (start us, length us, event | category | flops | bytes accessed | tf_op | source)
XLA Modules:
  0.0 88.5 jit_solution(17178915491773171486)
XLA Ops:
  0.6 84.3 %shard_map.157 = (bf16[8,16,2,16,128]{4,3,2,1,0:T(8,128)(2,1)}, f32[2,8,4,512]{3,2,1,0:T(4,128)}) custom-call(bf16[128,4096]{1,0:T(8,128)(2,1)} %inputs.1, bf16[3,8,16,2,16,128]{5,4,3,2,1,0:T(8,128)(2,1)} %bitcast.2, f32[3,3,4096]{2,1,0:T(4,128)} %taps.1, f32[32,16384]{1,0:T(8,128)} %filters.1, f32[32]{0:T(128)} %gain.1, ...), custom_call_target="tpu_custom_call" | custom-call | tf_op jit(solution)/shard_map/pallas_call | solution.py:523
  84.9 3.6 %shard_map.158 = (bf16[8,16,2,16,128]{4,3,2,1,0:T(8,128)(2,1)}, f32[4,8,512]{2,1,0:T(8,128)}, f32[4,8,512]{2,1,0:T(8,128)}) custom-call(bf16[8,16,2,16,128]{4,3,2,1,0:T(8,128)(2,1)} %get-tuple-element.8.got, f32[2,8,4,512]{3,2,1,0:T(4,128)} %get-tuple-element.9.sums), custom_call_target="tpu_custom_call" | custom-call | tf_op jit(solution)/shard_map/pallas_call | solution.py:570

commit v3 on v2

--- a/solution.py
+++ b/solution.py
@@ -18,7 +18,7 @@
 HALF = OWN // 2
 SIDE = 128
 PAIRS = 2
-EARLY = 4
+CONSTANTS = 9
 F32 = jnp.float32
 BF16 = jnp.bfloat16
 MESH = pl.DeviceIdType.MESH
@@ -83,18 +83,22 @@
 
 
 def kernel(
-    inputs, streams, taps, filters, gain, one_x, one_h, two_x, two_y, one_y, turn_re, turn_im, pick, shift,
-    gated, sums,
+    inputs, streams, taps, filters, gain, *rest
+):
+    constants, rest = rest[:CONSTANTS], rest[CONSTANTS:]
+    local, rest = rest[-CONSTANTS:], rest[:-CONSTANTS]
+    one_x, one_h, two_x, two_y, one_y, turn_re, turn_im, pick, shift = local
+    (gated, sums,
     x_own, h_own, taps_rows, taps_cols, edge_out, edge_in, edge_wide,
     p_out, p_in, q_out, q_in, i_in,
     r_in, r_rows, h_rows, h_spec, y_rows, y_out, c_in,
     g_out, g_cols, part_out, part_in, fin_out,
-    local_sem, edge_sem, group_send, group_recv, block_send, block_recv, fin_send, fin_recv,
-):
+    local_sem, edge_sem, group_send, group_recv, block_send, block_recv, fin_send, fin_recv, constant_sem) = rest
     me = lax.axis_index("ctx")
     block = lax.div(me, 16)
     place = lax.rem(me, 16)
     group = 8 * lax.rem(lax.div(place, 8) + block, 2) + lax.rem(place, 8)
+    line, spot = lax.div(me, 8), lax.rem(me, 8)
 
     def member(b, j):
         return 16 * b + 8 * lax.rem(lax.div(j, 8) + b, 2) + lax.rem(j, 8)
@@ -104,11 +108,8 @@
             src_ref=src, dst_ref=dst, send_sem=send, recv_sem=recv, device_id=(device,), device_id_type=MESH
         )
 
-    def other_blocks(first=1, last=BLOCKS):
-        def loop(step):
-            pl.loop(first, last)(lambda r: step(lax.rem(block + r, BLOCKS)))
-
-        return loop
+    def other_blocks(step):
+        pl.loop(1, BLOCKS)(lambda r: step(lax.rem(block + r, BLOCKS)))
 
     def other_places(step):
         pl.loop(1, PLACES)(lambda r: step(lax.rem(place + r, PLACES)))
@@ -116,13 +117,20 @@
     def other_groups(step):
         pl.loop(1, PLACES)(lambda r: step(lax.rem(group + r, PLACES)))
 
+    def other_lines(step):
+        pl.loop(1, PLACES)(lambda r: step(lax.rem(line + r, PLACES)))
+
+    def other_spots(step):
+        pl.loop(1, BLOCKS)(lambda r: step(lax.rem(spot + r, BLOCKS)))
+
     barrier = pltpu.get_barrier_semaphore()
 
     def greet(device):
         pl.semaphore_signal(barrier, inc=1, device_id=(device,), device_id_type=MESH)
 
-    other_blocks()(lambda u: greet(member(u, group)))
+    other_blocks(lambda u: greet(member(u, group)))
     other_places(lambda o: greet(16 * block + o))
+    other_lines(lambda n: greet(8 * n + spot))
     greet(lax.rem(me + 1, DEVICES))
     greet(lax.rem(me + DEVICES - 1, DEVICES))
 
@@ -139,8 +147,16 @@
     stream_copies = [
         pltpu.make_async_copy(streams.at[s], x_own.at[s], local_sem.at[s]) for s in range(SHORT)
     ]
-    for s in (1, 2, 0):
-        stream_copies[s].start()
+    constant_copies = [
+        pltpu.make_async_copy(constants[k], local[k], constant_sem.at[k]) for k in range(CONSTANTS)
+    ]
+    stream_copies[1].start()
+    stream_copies[2].start()
+    constant_copies[-1].start()
+    constant_copies[-2].start()
+    stream_copies[0].start()
+    for copy in constant_copies[:-2]:
+        copy.start()
     filter_copy = pltpu.make_async_copy(filters, h_own, local_sem.at[3])
     filter_copy.start()
 
@@ -172,25 +188,27 @@
                     edge += pltpu.roll(got, at, 1) if at else got
         edge_out[which] = edge.astype(BF16)
 
+    constant_copies[-1].wait()
+    constant_copies[-2].wait()
     stream_copies[1].wait()
     stream_copies[2].wait()
     fill_edge(0, 4)
 
-    pl.semaphore_wait(barrier, 2 + BLOCKS - 1 + PLACES - 1 + 2 * BLOCKS - 2 * jnp.where(lax.div(me, 8) == place, 1, 0))
+    pl.semaphore_wait(barrier, 2 + BLOCKS - 1 + 2 * (PLACES - 1) + 2 * BLOCKS - 2 * jnp.where(lax.div(me, 8) == place, 1, 0))
 
     @pl.when(me < DEVICES - 1)
     def _():
         edge_copy(0).start()
 
-    def columns(u):
-        return pl.ds(pl.multiple_of(u * BLOCK, BLOCK), BLOCK)
-
-    def input_copy(u, slot):
-        return remote(inputs.at[:, columns(u)], i_in.at[slot], group_send.at[2, u], group_recv.at[2, slot], member(u, group))
-
-    own_input = pltpu.make_async_copy(inputs.at[:, columns(block)], i_in.at[block], local_sem.at[4])
+    def columns(b):
+        return pl.ds(pl.multiple_of(b * BLOCK, BLOCK), BLOCK)
+
+    def input_copy(b, slot):
+        return remote(inputs.at[:, columns(b)], i_in.at[slot], group_send.at[2, b], group_recv.at[2, slot], 8 * line + b)
+
+    own_input = pltpu.make_async_copy(inputs.at[:, columns(spot)], i_in.at[spot], local_sem.at[4])
     own_input.start()
-    other_blocks(1, EARLY)(lambda u: input_copy(u, block).start())
+    other_spots(lambda b: input_copy(b, spot).start())
 
     stream_copies[0].wait()
     fill_edge(1, 2)
@@ -248,7 +266,7 @@
     take_edge(0)
 
     for h in range(2):
-        @other_blocks()
+        @other_blocks
         def _(u):
             fill_product(p_out.at[u, h], u, h)
             product_copy(u, block, h).start()
@@ -257,13 +275,14 @@
 
     take_edge(1)
 
-    @other_blocks()
+    @other_blocks
     def _(u):
         fill_query(q_out.at[u], u)
         query_copy(u, block).start()
 
     fill_query(q_in.at[block], block)
-    other_blocks(EARLY)(lambda u: input_copy(u, block).start())
+    for copy in constant_copies[:-2]:
+        copy.wait()
 
     def pair(ref, c, stride):
         return [ref[pl.ds(c + k, SIDE, stride=stride), :] for k in range(2)]
@@ -300,7 +319,7 @@
         return pltpu.make_async_copy(p_in.at[:, h, place], r_in.at[h, group], local_sem.at[5 + h])
 
     def forward(h):
-        other_blocks()(lambda u: product_copy(u, u, h).wait_recv())
+        other_blocks(lambda u: product_copy(u, u, h).wait_recv())
         other_places(lambda o: owner_copy(o, group, h).start())
         own_product(h).start()
 
@@ -364,26 +383,27 @@
     def part_rows(o):
         return pl.ds(pl.multiple_of(o * OWN, OWN), OWN)
 
-    def part_copy(which, o, slot):
-        return remote(
-            part_out.at[which, part_rows(o), :],
-            part_in.at[which, slot],
-            block_send.at[4 + which, o],
-            block_recv.at[4 + which, slot],
-            16 * block + o,
-        )
-
-    def send_parts(which):
-        other_places(lambda o: part_copy(which, o, place).start())
-        part_in[which, place] = part_out[which, part_rows(place), :]
-
-    def fin_copy(which, i, slot, device):
-        return remote(
-            fin_out.at[which, i], sums.at[which, slot], fin_send.at[which, i], fin_recv.at[which, slot], device
+    def input_part(n, slot):
+        return remote(
+            part_out.at[0, part_rows(n), :], part_in.at[0, slot], block_send.at[4, n], block_recv.at[4, slot], 8 * n + spot
+        )
+
+    def output_part(o, slot):
+        return remote(
+            part_out.at[1, part_rows(o), :], part_in.at[1, slot], block_send.at[5, o], block_recv.at[5, slot], 16 * block + o
+        )
+
+    def input_sum(i, slot):
+        return remote(
+            fin_out.at[0, i], sums.at[0, slot], fin_send.at[0, i], fin_recv.at[0, slot], 8 * line + i
+        )
+
+    def output_sum(i, slot, device):
+        return remote(
+            fin_out.at[1, i], sums.at[1, slot], fin_send.at[1, i], fin_recv.at[1, slot], device
         )
 
     def sum_parts(which):
-        other_places(lambda o: part_copy(which, o, o).wait_recv())
         total = part_in[which, 0].astype(F32)
         for o in range(1, PLACES):
             total += part_in[which, o].astype(F32)
@@ -391,37 +411,51 @@
         for i in range(BLOCKS):
             fin_out[which, i] = total[4 * i : 4 * i + 4]
 
+    def send_input_parts():
+        other_lines(lambda n: input_part(n, line).start())
+        part_in[0, line] = part_out[0, part_rows(line), :]
+
+    def send_input_sums():
+        other_lines(lambda n: input_part(n, n).wait_recv())
+        sum_parts(0)
+        other_spots(lambda i: input_sum(i, spot).start())
+        sums[0, spot] = fin_out[0, spot]
+
+    def send_output_parts():
+        other_places(lambda o: output_part(o, place).start())
+        part_in[1, place] = part_out[1, part_rows(place), :]
+
+    def send_output_sums():
+        other_places(lambda o: output_part(o, o).wait_recv())
+        sum_parts(1)
+
         @pl.loop(0, BLOCKS)
         def _(i):
             device = 8 * place + i
 
             @pl.when(device != me)
             def _():
-                fin_copy(which, i, block, device).start()
+                output_sum(i, block, device).start()
 
             @pl.when(device == me)
             def _():
-                sums[which, block] = fin_out[which, i]
-
-    def wait_fin(which):
+                sums[1, block] = fin_out[1, i]
+
+    def wait_sums():
+        other_spots(lambda b: input_sum(b, b).wait_recv())
+
         @pl.loop(0, BLOCKS)
         def _(b):
-            @pl.when(16 * b + lax.div(me, 8) != me)
+            @pl.when(16 * b + line != me)
             def _():
-                fin_copy(which, 0, b, me).wait_recv()
-
+                output_sum(0, b, me).wait_recv()
+
+    forward(0)
     filter_half(0)
-    forward(0)
+    forward(1)
     filter_half(1)
-    forward(1)
     convolve(0)
     convolve(1)
-
-    own_input.wait()
-    other_blocks()(lambda u: input_copy(u, u).wait_recv())
-    rows = i_in[...].reshape(BLOCKS * SIDE, BLOCK)
-    part_out[0] = dot(rows, rows, ((0,), (0,))).astype(BF16)
-    send_parts(0)
 
     def gated_copy(u, slot, h):
         return remote(
@@ -436,44 +470,59 @@
         g_out[u, h] = value
         g_cols[:, h, :, pl.ds(pl.multiple_of(u * SIDE, SIDE), SIDE)] = value
 
-    other_blocks()(lambda u: query_copy(u, u).wait_recv())
-
-    for h in range(2):
+    other_blocks(lambda u: query_copy(u, u).wait_recv())
+
+    def wait_conv(h):
         other_places(lambda o: conv_copy(group, o, h).wait_recv())
 
-        @other_blocks()
-        def _(u):
-            fill_gated(u, h)
-            gated_copy(u, block, h).start()
-
-        fill_gated(block, h)
-        own_gated(h).start()
-
+    wait_conv(0)
+
+    @other_blocks
+    def _(u):
+        fill_gated(u, 0)
+        gated_copy(u, block, 0).start()
+
+    fill_gated(block, 0)
+    own_gated(0).start()
+    own_input.wait()
+    other_spots(lambda b: input_copy(b, b).wait_recv())
+    rows = i_in[...].reshape(BLOCKS * SIDE, BLOCK)
+    part_out[0] = dot(rows, rows, ((0,), (0,))).astype(BF16)
+    send_input_parts()
+    wait_conv(1)
+    pl.loop(0, BLOCKS)(lambda u: fill_gated(u, 1))
     columns_all = g_cols[...].reshape(BLOCK, BLOCKS * SIDE)
     part_out[1] = dot(columns_all, columns_all, ((1,), (1,))).astype(BF16)
-    send_parts(1)
-    sum_parts(0)
-    sum_parts(1)
-    wait_fin(0)
-    wait_fin(1)
+    send_output_parts()
+    other_blocks(lambda u: gated_copy(u, block, 1).start())
+    own_gated(1).start()
+    send_input_sums()
+    send_output_sums()
+    wait_sums()
 
     for h in range(2):
         own_gated(h).wait()
 
-    @other_blocks()
+    @other_blocks
     def _(u):
         for h in range(2):
             gated_copy(u, u, h).wait_recv()
             gated_copy(u, u, h).wait_send()
             product_copy(u, u, h).wait_send()
         query_copy(u, u).wait_send()
-        input_copy(u, u).wait_send()
+
+    @other_spots
+    def _(b):
+        input_copy(b, b).wait_send()
+        input_sum(b, b).wait_send()
+
+    other_lines(lambda n: input_part(n, n).wait_send())
 
     @other_places
     def _(o):
         for h in range(2):
             owner_copy(o, o, h).wait_send()
-            part_copy(h, o, o).wait_send()
+        output_part(o, o).wait_send()
 
     @other_groups
     def _(j):
@@ -484,8 +533,7 @@
     def _(i):
         @pl.when(8 * place + i != me)
         def _():
-            for which in range(2):
-                fin_copy(which, i, i, me).wait_send()
+            output_sum(i, i, me).wait_send()
 
     @pl.when(me < DEVICES - 1)
     def _():
@@ -526,7 +574,7 @@
             jax.ShapeDtypeStruct((BLOCKS, PLACES, 2, HALF, SIDE), BF16),
             jax.ShapeDtypeStruct((2, BLOCKS, rows, BLOCK), F32),
         ),
-        in_specs=[anywhere, anywhere, vmem, anywhere, smem] + [vmem] * len(constants),
+        in_specs=[anywhere, anywhere, vmem, anywhere, smem] + [anywhere] * CONSTANTS,
         out_specs=(anywhere, vmem),
         scratch_shapes=[
             pltpu.VMEM((SHORT, BLOCKS, PLACES, 2, HALF, SIDE), BF16),
@@ -561,7 +609,9 @@
             dma((6, PLACES)),
             dma((2, BLOCKS)),
             dma((2, BLOCKS)),
-        ],
+            dma((CONSTANTS,)),
+        ]
+        + [pltpu.VMEM(c.shape, c.dtype) for c in constants],
         compiler_params=pltpu.CompilerParams(
             collective_id=0, has_side_effects=True, vmem_limit_bytes=56 * 1024 * 1024
         ),

time: 88.7 us -> 83.5 us (0.941)
  Pallas kernels: 87.9 us -> 82.6 us
    pallas_call x1, Pallas kernels: 84.3 us -> 79 us  [body(): pl.pallas_call(kernel, out_shape=(jax.ShapeDtypeStruct((BLOCKS, PLACES, 2...]
where the time goes in v3:
time: 83.5 us; the launch traced here: 83.3 us
  Pallas kernels  82.6 us (99%)
    pallas_call x1, Pallas kernels, body(): pl.pallas_call(kernel, out_shape=(jax.ShapeDtypeStruct((BLOCKS, PLACES, 2...  79 us
    pallas_call x1, Pallas kernels, body(): pl.pallas_call(write_kernel, out_shape=(jax.ShapeDtypeStruct((BLOCKS, PLA...  3.64 us

profile of v3, /device:TPU:1, one launch (start us, length us, event | category | flops | bytes accessed | tf_op | source)
XLA Modules:
  0.0 83.3 jit_solution(12741210847347846730)
XLA Ops:
  0.6 79.0 %shard_map.157 = (bf16[8,16,2,16,128]{4,3,2,1,0:T(8,128)(2,1)}, f32[2,8,4,512]{3,2,1,0:T(4,128)}) custom-call(bf16[128,4096]{1,0:T(8,128)(2,1)} %inputs.1, bf16[3,8,16,2,16,128]{5,4,3,2,1,0:T(8,128)(2,1)} %bitcast.2, f32[3,3,4096]{2,1,0:T(4,128)} %taps.1, f32[32,16384]{1,0:T(8,128)} %filters.1, f32[32]{0:T(128)} %gain.1, ...), custom_call_target="tpu_custom_call" | custom-call | tf_op jit(solution)/shard_map/pallas_call | solution.py:571
  79.6 3.6 %shard_map.158 = (bf16[8,16,2,16,128]{4,3,2,1,0:T(8,128)(2,1)}, f32[4,8,512]{2,1,0:T(8,128)}, f32[4,8,512]{2,1,0:T(8,128)}) custom-call(bf16[8,16,2,16,128]{4,3,2,1,0:T(8,128)(2,1)} %get-tuple-element.8.got, f32[2,8,4,512]{3,2,1,0:T(4,128)} %get-tuple-element.9.sums), custom_call_target="tpu_custom_call" | custom-call | tf_op jit(solution)/shard_map/pallas_call | solution.py:620

commit v4 on v3

--- a/solution.py
+++ b/solution.py
@@ -17,8 +17,8 @@
 OWN = D // DEVICES
 HALF = OWN // 2
 SIDE = 128
-PAIRS = 2
-CONSTANTS = 9
+PAIRS = 4
+CONSTANTS = 10
 F32 = jnp.float32
 BF16 = jnp.bfloat16
 MESH = pl.DeviceIdType.MESH
@@ -64,7 +64,9 @@
         shift[s, index[:-1], index[1:]] = 1
         shift[s, index[:-2], SIDE + index[2:]] = 1
         shift[s, at + 1, 0] = shift[s, at, SIDE] = shift[s, at + 1, SIDE + 1] = 1
-    return one_x, one_h, two_x, two_y, one_y, turn_re, turn_im, pick.astype(BF16), shift.astype(BF16)
+    rows = np.arange(BLOCK).reshape(BLOCKS, PLACES, BLOCK // DEVICES).swapaxes(0, 1).reshape(-1)
+    order = np.eye(BLOCK)[rows].astype(BF16)
+    return one_x, one_h, two_x, two_y, one_y, turn_re, turn_im, order, pick.astype(BF16), shift.astype(BF16)
 
 
 def halves(values):
@@ -87,7 +89,7 @@
 ):
     constants, rest = rest[:CONSTANTS], rest[CONSTANTS:]
     local, rest = rest[-CONSTANTS:], rest[:-CONSTANTS]
-    one_x, one_h, two_x, two_y, one_y, turn_re, turn_im, pick, shift = local
+    one_x, one_h, two_x, two_y, one_y, turn_re, turn_im, order, pick, shift = local
     (gated, sums,
     x_own, h_own, taps_rows, taps_cols, edge_out, edge_in, edge_wide,
     p_out, p_in, q_out, q_in, i_in,
@@ -134,15 +136,7 @@
     greet(lax.rem(me + 1, DEVICES))
     greet(lax.rem(me + DEVICES - 1, DEVICES))
 
-    @pl.loop(0, BLOCKS)
-    def _(i):
-        @pl.when(8 * place + i != me)
-        def _():
-            greet(8 * place + i)
-
-        @pl.when(16 * i + lax.div(me, 8) != me)
-        def _():
-            greet(16 * i + lax.div(me, 8))
+    other_blocks(lambda u: greet(16 * u + place))
 
     stream_copies = [
         pltpu.make_async_copy(streams.at[s], x_own.at[s], local_sem.at[s]) for s in range(SHORT)
@@ -194,7 +188,7 @@
     stream_copies[2].wait()
     fill_edge(0, 4)
 
-    pl.semaphore_wait(barrier, 2 + BLOCKS - 1 + 2 * (PLACES - 1) + 2 * BLOCKS - 2 * jnp.where(lax.div(me, 8) == place, 1, 0))
+    pl.semaphore_wait(barrier, 2 + 2 * (BLOCKS - 1) + 2 * (PLACES - 1))
 
     @pl.when(me < DEVICES - 1)
     def _():
@@ -398,9 +392,9 @@
             fin_out.at[0, i], sums.at[0, slot], fin_send.at[0, i], fin_recv.at[0, slot], 8 * line + i
         )
 
-    def output_sum(i, slot, device):
-        return remote(
-            fin_out.at[1, i], sums.at[1, slot], fin_send.at[1, i], fin_recv.at[1, slot], device
+    def output_sum(b, slot):
+        return remote(
+            fin_out.at[1, b], sums.at[1, slot], fin_send.at[1, b], fin_recv.at[1, slot], 16 * b + place
         )
 
     def sum_parts(which):
@@ -428,27 +422,12 @@
     def send_output_sums():
         other_places(lambda o: output_part(o, o).wait_recv())
         sum_parts(1)
-
-        @pl.loop(0, BLOCKS)
-        def _(i):
-            device = 8 * place + i
-
-            @pl.when(device != me)
-            def _():
-                output_sum(i, block, device).start()
-
-            @pl.when(device == me)
-            def _():
-                sums[1, block] = fin_out[1, i]
+        other_blocks(lambda b: output_sum(b, block).start())
+        sums[1, block] = fin_out[1, block]
 
     def wait_sums():
         other_spots(lambda b: input_sum(b, b).wait_recv())
-
-        @pl.loop(0, BLOCKS)
-        def _(b):
-            @pl.when(16 * b + line != me)
-            def _():
-                output_sum(0, b, me).wait_recv()
+        other_blocks(lambda b: output_sum(b, b).wait_recv())
 
     forward(0)
     filter_half(0)
@@ -492,7 +471,8 @@
     wait_conv(1)
     pl.loop(0, BLOCKS)(lambda u: fill_gated(u, 1))
     columns_all = g_cols[...].reshape(BLOCK, BLOCKS * SIDE)
-    part_out[1] = dot(columns_all, columns_all, ((1,), (1,))).astype(BF16)
+    part = dot(columns_all, columns_all, ((1,), (1,))).astype(BF16)
+    part_out[1] = dot(order[...], part).astype(BF16)
     send_output_parts()
     other_blocks(lambda u: gated_copy(u, block, 1).start())
     own_gated(1).start()
@@ -510,6 +490,7 @@
             gated_copy(u, u, h).wait_send()
             product_copy(u, u, h).wait_send()
         query_copy(u, u).wait_send()
+        output_sum(u, u).wait_send()
 
     @other_spots
     def _(b):
@@ -528,12 +509,6 @@
     def _(j):
         for h in range(2):
             conv_copy(j, j, h).wait_send()
-
-    @pl.loop(0, BLOCKS)
-    def _(i):
-        @pl.when(8 * place + i != me)
-        def _():
-            output_sum(i, i, me).wait_send()
 
     @pl.when(me < DEVICES - 1)
     def _():

time: 83.5 us -> 79.3 us (0.950)
  Pallas kernels: 82.6 us -> 78.5 us
    pallas_call x1, Pallas kernels: 79 us -> 74.9 us  [body(): pl.pallas_call(kernel, out_shape=(jax.ShapeDtypeStruct((BLOCKS, PLACES, 2...]
where the time goes in v4:
time: 79.3 us; the launch traced here: 79.1 us
  Pallas kernels  78.5 us (99%)
    pallas_call x1, Pallas kernels, body(): pl.pallas_call(kernel, out_shape=(jax.ShapeDtypeStruct((BLOCKS, PLACES, 2...  74.9 us
    pallas_call x1, Pallas kernels, body(): pl.pallas_call(write_kernel, out_shape=(jax.ShapeDtypeStruct((BLOCKS, PLA...  3.64 us

profile of v4, /device:TPU:1, one launch (start us, length us, event | category | flops | bytes accessed | tf_op | source)
XLA Modules:
  0.0 79.1 jit_solution(8399314745848279441)
XLA Ops:
  0.6 74.9 %shard_map.166 = (bf16[8,16,2,16,128]{4,3,2,1,0:T(8,128)(2,1)}, f32[2,8,4,512]{3,2,1,0:T(4,128)}) custom-call(bf16[128,4096]{1,0:T(8,128)(2,1)} %inputs.1, bf16[3,8,16,2,16,128]{5,4,3,2,1,0:T(8,128)(2,1)} %bitcast.2, f32[3,3,4096]{2,1,0:T(4,128)} %taps.1, f32[32,16384]{1,0:T(8,128)} %filters.1, f32[32]{0:T(128)} %gain.1, ...), custom_call_target="tpu_custom_call" | custom-call | tf_op jit(solution)/shard_map/pallas_call | solution.py:546
  75.5 3.6 %shard_map.167 = (bf16[8,16,2,16,128]{4,3,2,1,0:T(8,128)(2,1)}, f32[4,8,512]{2,1,0:T(8,128)}, f32[4,8,512]{2,1,0:T(8,128)}) custom-call(bf16[8,16,2,16,128]{4,3,2,1,0:T(8,128)(2,1)} %get-tuple-element.8.got, f32[2,8,4,512]{3,2,1,0:T(4,128)} %get-tuple-element.9.sums), custom_call_target="tpu_custom_call" | custom-call | tf_op jit(solution)/shard_map/pallas_call | solution.py:595

commit v5 on v4

--- a/solution.py
+++ b/solution.py
@@ -187,12 +187,15 @@
     stream_copies[1].wait()
     stream_copies[2].wait()
     fill_edge(0, 4)
+    stream_copies[0].wait()
+    fill_edge(1, 2)
 
     pl.semaphore_wait(barrier, 2 + 2 * (BLOCKS - 1) + 2 * (PLACES - 1))
 
     @pl.when(me < DEVICES - 1)
     def _():
         edge_copy(0).start()
+        edge_copy(1).start()
 
     def columns(b):
         return pl.ds(pl.multiple_of(b * BLOCK, BLOCK), BLOCK)
@@ -204,12 +207,6 @@
     own_input.start()
     other_spots(lambda b: input_copy(b, spot).start())
 
-    stream_copies[0].wait()
-    fill_edge(1, 2)
-
-    @pl.when(me < DEVICES - 1)
-    def _():
-        edge_copy(1).start()
 
     filter_copy.wait()
     for m in range(SIDE):
@@ -272,7 +269,6 @@
     @other_blocks
     def _(u):
         fill_query(q_out.at[u], u)
-        query_copy(u, block).start()
 
     fill_query(q_in.at[block], block)
     for copy in constant_copies[:-2]:
@@ -432,6 +428,7 @@
     forward(0)
     filter_half(0)
     forward(1)
+    other_blocks(lambda u: query_copy(u, block).start())
     filter_half(1)
     convolve(0)
     convolve(1)

time: 79.3 us -> 77.2 us (0.974)
  Pallas kernels: 78.5 us -> 76.2 us
    pallas_call x1, Pallas kernels: 74.9 us -> 72.6 us  [body(): pl.pallas_call(kernel, out_shape=(jax.ShapeDtypeStruct((BLOCKS, PLACES, 2...]
where the time goes in v5:
time: 77.2 us; the launch traced here: 76.9 us
  Pallas kernels  76.2 us (99%)
    pallas_call x1, Pallas kernels, body(): pl.pallas_call(kernel, out_shape=(jax.ShapeDtypeStruct((BLOCKS, PLACES, 2...  72.6 us
    pallas_call x1, Pallas kernels, body(): pl.pallas_call(write_kernel, out_shape=(jax.ShapeDtypeStruct((BLOCKS, PLA...  3.64 us

profile of v5, /device:TPU:1, one launch (start us, length us, event | category | flops | bytes accessed | tf_op | source)
XLA Modules:
  0.0 76.9 jit_solution(7133907536457391230)
XLA Ops:
  0.6 72.6 %shard_map.166 = (bf16[8,16,2,16,128]{4,3,2,1,0:T(8,128)(2,1)}, f32[2,8,4,512]{3,2,1,0:T(4,128)}) custom-call(bf16[128,4096]{1,0:T(8,128)(2,1)} %inputs.1, bf16[3,8,16,2,16,128]{5,4,3,2,1,0:T(8,128)(2,1)} %bitcast.2, f32[3,3,4096]{2,1,0:T(4,128)} %taps.1, f32[32,16384]{1,0:T(8,128)} %filters.1, f32[32]{0:T(128)} %gain.1, ...), custom_call_target="tpu_custom_call" | custom-call | tf_op jit(solution)/shard_map/pallas_call | solution.py:543
  73.2 3.6 %shard_map.167 = (bf16[8,16,2,16,128]{4,3,2,1,0:T(8,128)(2,1)}, f32[4,8,512]{2,1,0:T(8,128)}, f32[4,8,512]{2,1,0:T(8,128)}) custom-call(bf16[8,16,2,16,128]{4,3,2,1,0:T(8,128)(2,1)} %get-tuple-element.8.got, f32[2,8,4,512]{3,2,1,0:T(4,128)} %get-tuple-element.9.sums), custom_call_target="tpu_custom_call" | custom-call | tf_op jit(solution)/shard_map/pallas_call | solution.py:592

commit v6 on v5

--- a/solution.py
+++ b/solution.py
@@ -17,7 +17,7 @@
 OWN = D // DEVICES
 HALF = OWN // 2
 SIDE = 128
-PAIRS = 4
+PAIRS = 8
 CONSTANTS = 10
 F32 = jnp.float32
 BF16 = jnp.bfloat16
@@ -111,19 +111,19 @@
         )
 
     def other_blocks(step):
-        pl.loop(1, BLOCKS)(lambda r: step(lax.rem(block + r, BLOCKS)))
+        pl.loop(1, BLOCKS, unroll=True)(lambda r: step(lax.rem(block + r, BLOCKS)))
 
     def other_places(step):
-        pl.loop(1, PLACES)(lambda r: step(lax.rem(place + r, PLACES)))
+        pl.loop(1, PLACES, unroll=True)(lambda r: step(lax.rem(place + r, PLACES)))
 
     def other_groups(step):
-        pl.loop(1, PLACES)(lambda r: step(lax.rem(group + r, PLACES)))
+        pl.loop(1, PLACES, unroll=True)(lambda r: step(lax.rem(group + r, PLACES)))
 
     def other_lines(step):
-        pl.loop(1, PLACES)(lambda r: step(lax.rem(line + r, PLACES)))
+        pl.loop(1, PLACES, unroll=True)(lambda r: step(lax.rem(line + r, PLACES)))
 
     def other_spots(step):
-        pl.loop(1, BLOCKS)(lambda r: step(lax.rem(spot + r, BLOCKS)))
+        pl.loop(1, BLOCKS, unroll=True)(lambda r: step(lax.rem(spot + r, BLOCKS)))
 
     barrier = pltpu.get_barrier_semaphore()
 
@@ -465,6 +465,24 @@
     rows = i_in[...].reshape(BLOCKS * SIDE, BLOCK)
     part_out[0] = dot(rows, rows, ((0,), (0,))).astype(BF16)
     send_input_parts()
+    @other_blocks
+    def _(u):
+        for h in range(2):
+            product_copy(u, u, h).wait_send()
+        query_copy(u, u).wait_send()
+
+    @other_places
+    def _(o):
+        for h in range(2):
+            owner_copy(o, o, h).wait_send()
+
+    other_spots(lambda b: input_copy(b, b).wait_send())
+
+    @pl.when(me < DEVICES - 1)
+    def _():
+        for which in range(2):
+            edge_copy(which).wait_send()
+
     wait_conv(1)
     pl.loop(0, BLOCKS)(lambda u: fill_gated(u, 1))
     columns_all = g_cols[...].reshape(BLOCK, BLOCKS * SIDE)
@@ -485,32 +503,16 @@
         for h in range(2):
             gated_copy(u, u, h).wait_recv()
             gated_copy(u, u, h).wait_send()
-            product_copy(u, u, h).wait_send()
-        query_copy(u, u).wait_send()
         output_sum(u, u).wait_send()
 
-    @other_spots
-    def _(b):
-        input_copy(b, b).wait_send()
-        input_sum(b, b).wait_send()
-
+    other_spots(lambda b: input_sum(b, b).wait_send())
     other_lines(lambda n: input_part(n, n).wait_send())
-
-    @other_places
-    def _(o):
-        for h in range(2):
-            owner_copy(o, o, h).wait_send()
-        output_part(o, o).wait_send()
+    other_places(lambda o: output_part(o, o).wait_send())
 
     @other_groups
     def _(j):
         for h in range(2):
             conv_copy(j, j, h).wait_send()
-
-    @pl.when(me < DEVICES - 1)
-    def _():
-        for which in range(2):
-            edge_copy(which).wait_send()
 
 
 def write_kernel(got, sums, gated, input_gram, output_gram, held, sems):

time: 77.2 us -> 75.5 us (0.978)
  Pallas kernels: 76.2 us -> 74.5 us
    pallas_call x1, Pallas kernels: 72.6 us -> 70.9 us  [body(): pl.pallas_call(kernel, out_shape=(jax.ShapeDtypeStruct((BLOCKS, PLACES, 2...]
where the time goes in v6:
time: 75.5 us; the launch traced here: 75.3 us
  Pallas kernels  74.5 us (99%)
  between operations  0.8 us (1%)
    pallas_call x1, Pallas kernels, body(): pl.pallas_call(kernel, out_shape=(jax.ShapeDtypeStruct((BLOCKS, PLACES, 2...  70.9 us
    pallas_call x1, Pallas kernels, body(): pl.pallas_call(write_kernel, out_shape=(jax.ShapeDtypeStruct((BLOCKS, PLA...  3.64 us

profile of v6, /device:TPU:1, one launch (start us, length us, event | category | flops | bytes accessed | tf_op | source)
XLA Modules:
  0.0 75.3 jit_solution(10171982308758962989)
XLA Ops:
  0.6 70.9 %shard_map.166 = (bf16[8,16,2,16,128]{4,3,2,1,0:T(8,128)(2,1)}, f32[2,8,4,512]{3,2,1,0:T(4,128)}) custom-call(bf16[128,4096]{1,0:T(8,128)(2,1)} %inputs.1, bf16[3,8,16,2,16,128]{5,4,3,2,1,0:T(8,128)(2,1)} %bitcast.2, f32[3,3,4096]{2,1,0:T(4,128)} %taps.1, f32[32,16384]{1,0:T(8,128)} %filters.1, f32[32]{0:T(128)} %gain.1, ...), custom_call_target="tpu_custom_call" | custom-call | tf_op jit(solution)/shard_map/pallas_call | solution.py:545
  71.5 3.6 %shard_map.167 = (bf16[8,16,2,16,128]{4,3,2,1,0:T(8,128)(2,1)}, f32[4,8,512]{2,1,0:T(8,128)}, f32[4,8,512]{2,1,0:T(8,128)}) custom-call(bf16[8,16,2,16,128]{4,3,2,1,0:T(8,128)(2,1)} %get-tuple-element.8.got, f32[2,8,4,512]{3,2,1,0:T(4,128)} %get-tuple-element.9.sums), custom_call_target="tpu_custom_call" | custom-call | tf_op jit(solution)/shard_map/pallas_call | solution.py:594
